TPU v7x, 32 devices: a whole 2x2x4 slice. The times are simulated.
32 devices in a mesh: rep: 4 (over x, core), fsdp: 8 (over z, y).
Axes of the slice: x: 2, y: 2, z: 4, core: 2. Of those that a mesh axis runs over, the one named last changes fastest.
Arguments:
- normed: bfloat16 [12288, 4608], P(('rep', 'fsdp')), may hold values from -6 to 6
- key_grad: bfloat16 [12288, 1024], P(('rep', 'fsdp')), may hold values from -6 to 6
- master: float32 [4, 4608, 1024], P('rep', 'fsdp'), may hold values from -6 to 6
- first_moment: float32 [4, 4608, 1024], P('rep', 'fsdp'), may hold values from -6 to 6
- second_moment: float32 [4, 4608, 1024], P('rep', 'fsdp'), may hold values from 0.1 to 10
- anchor: float32 [4608, 1024], P('fsdp'), may hold values from -6 to 6
- momentum: float32 [4608, 1024], P('fsdp'), may hold values from -6 to 6
- inner_step: int32 [1], replicated, may hold values from 1 to 6
Outputs:
- keys: bfloat16 [12288, 1024], P(('rep', 'fsdp'))
- input_grad: bfloat16 [12288, 4608], P(('rep', 'fsdp'))
- merged: float32 [4, 4608, 1024], P('rep', 'fsdp')
- new_first: float32 [4, 4608, 1024], P('rep', 'fsdp')
- new_second: float32 [4, 4608, 1024], P('rep', 'fsdp')
- new_anchor: float32 [4608, 1024], P('fsdp')
- new_momentum: float32 [4608, 1024], P('fsdp')
Inputs may be any that keep to these rules, and one draw needn't show every extreme that they name: `inner_step`: the 1-based count of inner steps taken by the inner optimizer.
All inputs are finite; a program needn't handle non-finite values.
Results may differ from a plain program's by a relative error of at most 0.0049.
Values may be sent and summed in bfloat16 or wider, within the bound.
No kernel may reach another device: no remote copies, remote signals or barrier semaphores. Data moves between devices by JAX's collectives and lax.ppermute only.
A program may use at most 128 MiB of HBM per device.

v0:
```python
import jax
import jax.numpy as jnp
from jax import lax
from jax.experimental import pallas as pl
from jax.experimental.pallas import tpu as pltpu
from jax.sharding import PartitionSpec as P

beta_first = 0.9
beta_second = 0.95
inner_rate = 0.1
weight_decay = 0.1
epsilon = 1e-08
outer_rate = 0.7
outer_mu = 0.9
mix_weight = 0.5

f32 = jnp.float32
bf16 = jnp.bfloat16
vmem_bytes = 16 * 1024 * 1024

expected = {
    "split": 30,
    "first part": 0,
    "input two": 12,
    "second part": 30,
    "nesterov": 1,
    "early own": 0,
    "early pair": 0,
    "handoff": 1,
    "input middle": 0,
    "join two": 0,
    "input far": 0,
    "input last": 12,
    "early sums": 1,
    "pair sums": 0,
    "late sums": 1,
    "own sums": 0,
    "join last": 0,
    "first half": 12,
}


def corrections(inner_step):
    count_float = inner_step[0].astype(f32)
    fix_first = 1.0 - jnp.power(f32(beta_first), count_float)
    fix_second = 1.0 - jnp.power(f32(beta_second), count_float)
    return fix_first, fix_second


def adam(gradient, local, first_old, second_old, fix_first, fix_second):
    first_new = beta_first * first_old + (1.0 - beta_first) * gradient
    second_new = beta_second * second_old + (1.0 - beta_second) * gradient * gradient
    direction = first_new / fix_first / (jnp.sqrt(second_new / fix_second) + epsilon)
    stepped = local - inner_rate * (direction + weight_decay * local)
    return (stepped, first_new, second_new)


def nesterov(outer_grad, anchor_rows, moment_rows):
    moment_new = outer_mu * moment_rows + outer_grad
    anchor_new = anchor_rows - outer_rate * (outer_grad + outer_mu * moment_new)
    return (anchor_new, moment_new)


def outer_update(local, anchor, momentum):
    summed = lax.psum(anchor - local, "rep")
    return nesterov(summed / lax.axis_size("rep"), anchor, momentum)


def whole_pass(normed, key_grad, local, first_old, second_old, anchor, momentum, inner_step):
    scale = normed.shape[1] ** (-0.5)
    weight = lax.all_gather(local.astype(bf16), "fsdp", axis=0, tiled=True)
    keys = (jnp.dot(normed, weight, preferred_element_type=f32) * scale).astype(bf16)
    input_grad = (
        lax.dot_general(key_grad, weight, (((1,), (1,)), ((), ())), preferred_element_type=f32)
        * scale
    ).astype(bf16)
    gradient = lax.psum_scatter(
        lax.dot_general(normed, key_grad, (((0,), (0,)), ((), ())), preferred_element_type=f32)
        * scale,
        "fsdp",
        scatter_dimension=0,
        tiled=True,
    )
    stepped, first_new, second_new = adam(
        gradient, local, first_old, second_old, *corrections(inner_step)
    )
    anchor_new, moment_new = outer_update(local, anchor, momentum)
    merged = mix_weight * stepped + (1.0 - mix_weight) * anchor_new
    return (keys, input_grad, merged, first_new, second_new, anchor_new, moment_new)


FAR, MIDDLE, BESIDE, OWN, Y, INNER, END, CORE = range(8)


class Order:
    def __init__(self, place):
        self.place = place
        self.token = None

    def call(self, kernel, inputs, outputs, grid, span=1, aliases=None, fixes=None):
        scalars = [self.place] + ([] if fixes is None else [fixes])
        tokens = [] if self.token is None else [self.token]
        before = len(scalars) + len(inputs)

        def wrapped(*refs):
            refs[-1][...] = jnp.zeros_like(refs[-1])
            kernel(*refs[:before], *refs[before + len(tokens) : -1])

        outputs = outputs + [whole(shaped(jnp.int32, 8, 128))]
        shapes = [shape for shape, _, _ in outputs]
        keep = pl.BlockSpec(memory_space=pl.ANY)
        out = pl.pallas_call(
            wrapped,
            out_shape=shapes,
            grid_spec=pltpu.PrefetchScalarGridSpec(
                num_scalar_prefetch=len(scalars),
                grid=grid,
                in_specs=[
                    keep if block is None else pl.BlockSpec(block, index)
                    for _, block, index in inputs
                ]
                + [keep] * len(tokens),
                out_specs=[pl.BlockSpec(block, index) for _, block, index in outputs],
            ),
            input_output_aliases=aliases or {},
            compiler_params=pltpu.CompilerParams(vmem_limit_bytes=vmem_bytes),
            cost_estimate=pl.CostEstimate(
                flops=int(span * 1e9), bytes_accessed=0, transcendentals=0
            ),
        )(*scalars, *[a for a, _, _ in inputs], *tokens)
        self.token = out[-1]
        return out[0] if len(out) == 2 else out[:-1]


def shaped(dtype, *shape):
    return jax.ShapeDtypeStruct(shape, dtype)


def whole(array):
    zeros = (0,) * len(array.shape)
    return (array, array.shape, lambda *_: zeros)


def rowwise(array, steps):
    return (array, (array.shape[0] // steps, array.shape[1]), lambda i, *_: (i, 0))


def columnwise(array, steps):
    return (array, (array.shape[0], array.shape[1] // steps), lambda i, *_: (0, i))


def stacked(array, k, rows):
    return (array, (rows, array.shape[1]), lambda *_: (k, 0))


def dot_t(a, b):
    return lax.dot_general(a, b, (((0,), (0,)), ((), ())), preferred_element_type=f32)


def dot_bt(a, b):
    return lax.dot_general(a, b, (((1,), (1,)), ((), ())), preferred_element_type=f32)


def dot(a, b):
    return jnp.dot(a, b, preferred_element_type=f32)


def chosen(flag, yes, no):
    return jnp.where(flag != 0, yes, no)


def halves(x_ref, rows):
    turned = x_ref[...].T
    return turned[:rows], turned[rows:]


def rounded(order, local):
    def kernel(s_ref, a_ref, out_ref):
        out_ref[...] = a_ref[...].astype(bf16)

    return order.call(
        kernel, [rowwise(local, 3)], [rowwise(shaped(bf16, *local.shape), 3)], (3,)
    )


def first_piece(order, normed, rows):
    tokens = normed.shape[0]

    def kernel(s_ref, x_ref, piece_ref):
        low, high = halves(x_ref, rows)
        piece_ref[...] = chosen(s_ref[Y], low, high)

    return order.call(
        kernel,
        [(normed, (tokens, 2 * rows), lambda i, s: (0, s[FAR]))],
        [whole(shaped(bf16, rows, tokens))],
        (1,),
    )


def split(order, normed, rows, g_pair, fixes):
    tokens = normed.shape[0]

    def kernel(s_ref, fix_ref, x_ref, g_ref, two_ref, last_ref, own_ref):
        i = pl.program_id(0)
        low, high = halves(x_ref, rows)
        own_ref[...] = chosen(s_ref[Y], high, low)

        @pl.when(i < 2)
        def _():
            two_ref[...] = chosen(s_ref[Y], low, high)

        @pl.when(i == 2)
        def _():
            last_ref[...] = chosen(s_ref[Y], low, high)

    return order.call(
        kernel,
        [
            (normed, (tokens, 2 * rows), lambda i, s, f: (0, s[(i + 1) % 4])),
            (g_pair, None, None),
        ],
        [
            (
                shaped(bf16, 2 * rows, tokens),
                (rows, tokens),
                lambda i, s, f: (jnp.minimum(i, 1), 0),
            ),
            (shaped(bf16, 3 * rows, tokens), (rows, tokens), lambda i, s, f: (0, 0)),
            (shaped(bf16, 4 * rows, tokens), (rows, tokens), lambda i, s, f: ((i + 1) % 4, 0)),
        ],
        (4,),
        expected["split"],
        fixes=fixes,
    )


def gradient_part(order, mine, k, theirs, at, key_grad, g_pair, scale, dtype, span):
    tokens, features = key_grad.shape
    rows = mine.shape[0] // 4

    def kernel(s_ref, x_ref, xp_ref, g_ref, gp_ref, out_ref):
        total = dot(x_ref[...], g_ref[...]) + dot(xp_ref[...], gp_ref[...])
        out_ref[...] = (total * scale).astype(dtype)

    return order.call(
        kernel,
        [
            stacked(mine, k, rows),
            stacked(theirs, at, rows),
            columnwise(key_grad, 2),
            columnwise(g_pair, 2),
        ],
        [columnwise(shaped(dtype, rows, features), 2)],
        (2,),
        span,
    )


def input_two(order, key_grad, g_pair, first, second, target, scale):
    tokens, features = key_grad.shape
    rows = first.shape[0]

    def kernel(s_ref, g_ref, gp_ref, a_ref, b_ref, target_ref, pair_ref, own_ref):
        weight = jnp.where(pl.program_id(0) == 0, a_ref[...], b_ref[...])
        pair_ref[...] = (dot_bt(weight, gp_ref[...]) * scale).astype(bf16)
        own_ref[...] = (dot_bt(weight, g_ref[...]) * scale).astype(bf16)

    return order.call(
        kernel,
        [whole(a) for a in (key_grad, g_pair, first, second)] + [(target, None, None)],
        [
            (target, (rows, tokens), lambda i, s: (1 + i, 0)),
            (shaped(bf16, 2 * rows, tokens), (rows, tokens), lambda i, s: (i, 0)),
        ],
        (2,),
        expected["input two"],
        {5: 0},
    )


def input_one(order, key_grad, g_pair, inner, part, end, scale, span, before=()):
    tokens, features = key_grad.shape
    rows = end.shape[0]

    def kernel(s_ref, g_ref, gp_ref, a_ref, b_ref, *rest):
        pair_ref, own_ref, w_ref = rest[len(before) :]
        weight = chosen(s_ref[INNER], a_ref[...], b_ref[...])
        w_ref[...] = weight
        pair_ref[...] = (dot_bt(weight, gp_ref[...]) * scale).astype(bf16)
        own_ref[...] = (dot_bt(weight, g_ref[...]) * scale).astype(bf16)

    out = whole(shaped(bf16, rows, tokens))
    return order.call(
        kernel,
        [whole(key_grad), whole(g_pair), stacked(inner, part, rows), whole(end)]
        + [(a, None, None) for a in before],
        [out, out, whole(shaped(bf16, rows, features))],
        (1,),
        span,
    )


def input_join(order, slots, own, others, shape, span, target=None, before=()):
    tokens = own[0][0][0].shape[1]
    tile = tokens // 3
    rows = shape[1] // 8
    flat = [
        (a, k, rows if len(piece) == 1 else a.shape[0]) for piece in own + others for a, k in piece
    ]
    kept = [a for a in (target, *before) if a is not None]

    def kernel(s_ref, *refs):
        values = iter([ref[...] for ref in refs[: len(flat)]])
        sides = [jnp.concatenate([next(values) for _ in piece], 0) for piece in own + others]
        first = pl.program_id(0) == 0
        mine = jnp.where(first, sides[0], sides[1])
        theirs = jnp.where(first, sides[2], sides[3])
        out_ref = refs[-1]

        @pl.when(s_ref[Y] == 0)
        def _():
            out_ref[...] = jnp.concatenate([mine, theirs], 0).T

        @pl.when(s_ref[Y] != 0)
        def _():
            out_ref[...] = jnp.concatenate([theirs, mine], 0).T

    def piece(array, k, height):
        return (array, (height, tile), lambda j, i, s: (k, i))

    return order.call(
        kernel,
        [piece(*p) for p in flat] + [(a, None, None) for a in kept],
        [(shaped(bf16, *shape), (tile, 2 * rows), lambda j, i, s: (i, s[slots[0] - j]))],
        (2, 3),
        span,
        None if target is None else {len(flat) + 1: 0},
    )


def key_sums(order, total, blocks, weights, span, scale=1.0, dtype=f32, before=()):
    features = weights[0].shape[1]
    tokens = blocks[0][0].shape[1]
    count = len(blocks)
    totals = [] if total is None else [columnwise(total, 2)]

    def kernel(s_ref, *refs):
        value = refs[2 * count][...] if totals else 0.0
        for x_ref, w_ref in zip(refs[:count], refs[count : 2 * count]):
            value += dot_t(x_ref[...], w_ref[...])
        refs[-1][...] = (value * scale).astype(dtype)

    return order.call(
        kernel,
        [stacked(x, k, w.shape[0]) for (x, k), w in zip(blocks, weights)]
        + [columnwise(w, 2) for w in weights]
        + totals
        + [(a, None, None) for a in before],
        [columnwise(shaped(dtype, tokens, features), 2)],
        (2,),
        span,
    )


def delta_halves(order, anchor, local):
    rows, features = local.shape

    def kernel(s_ref, a_ref, b_ref, c_ref, d_ref, own_ref, other_ref):
        own_ref[...] = a_ref[...] - b_ref[...]
        other_ref[...] = c_ref[...] - d_ref[...]

    def half(array, turned):
        def index(i, s):
            core = 1 - s[CORE] if turned else s[CORE]
            return (3 * core + i, 0)

        return (array, (rows // 6, features), index)

    out = rowwise(shaped(f32, rows // 2, features), 3)
    return order.call(
        kernel,
        [half(anchor, False), half(local, False), half(anchor, True), half(local, True)],
        [out, out],
        (3,),
    )


def total_of(order, here, there):
    def kernel(s_ref, a_ref, b_ref, out_ref):
        out_ref[...] = a_ref[...] + b_ref[...]

    return order.call(
        kernel, [rowwise(here, 3), rowwise(there, 3)], [rowwise(shaped(f32, *here.shape), 3)], (3,)
    )


def choose_sends(order, at_end, inside, beside):
    def kernel(s_ref, a_ref, b_ref, c_ref, out_ref, across_ref):
        out_ref[...] = chosen(s_ref[END], a_ref[...], b_ref[...])
        across_ref[...] = c_ref[...]

    out = rowwise(shaped(bf16, *inside.shape), 3)
    return order.call(
        kernel, [rowwise(a, 3) for a in (at_end, inside, beside)], [out, out], (3,), 0
    )


def first_handoff(order, p0, c1, p1, w_across):
    rows, features = p0.shape
    part = rows // 3

    def kernel(s_ref, p0_ref, c1_ref, p1_ref, w_ref, sum_a, send_a, sum_b, send_b):
        total = (p0_ref[...].astype(f32) + c1_ref[...].astype(f32)).astype(bf16)
        send = chosen(s_ref[END], p1_ref[...], w_ref[...])

        @pl.when(pl.program_id(0) < 2)
        def _():
            sum_a[...] = total
            send_a[...] = send

        @pl.when(pl.program_id(0) == 2)
        def _():
            sum_b[...] = total
            send_b[...] = send

    a = (
        shaped(bf16, 2 * part, features),
        (part, features),
        lambda i, s: (jnp.minimum(i, 1), 0),
    )
    b = whole(shaped(bf16, part, features))
    return order.call(
        kernel,
        [rowwise(x, 3) for x in (p0, c1, p1, w_across)],
        [a, a, b, b],
        (3,),
        expected["handoff"],
    )


def second_handoff(order, first, p1, c2, p2, q2, before, span):
    def kernel(s_ref, p1_ref, c2_ref, p2_ref, q2_ref, *rest):
        s1_ref, t_ref = rest[len(before) :]
        s1_ref[...] = (p1_ref[...].astype(f32) + c2_ref[...].astype(f32)).astype(bf16)
        t_ref[...] = (p2_ref[...] + q2_ref[...].astype(f32)).astype(bf16)

    sixth, features = p1.shape[0] // 6, p1.shape[1]
    steps = c2.shape[0] // sixth
    block = (sixth, features)
    out = rowwise(shaped(bf16, *c2.shape), steps)
    return order.call(
        kernel,
        [
            (p1, block, lambda i, s: (first + i, 0)),
            rowwise(c2, steps),
            (p2, block, lambda i, s: (first + i, 0)),
            rowwise(q2, steps),
        ]
        + [(a, None, None) for a in before],
        [out, out],
        (steps,),
        span,
    )


def nesterov_pass(order, own, other, anchor, momentum, local):
    rows, features = local.shape

    def kernel(s_ref, own_ref, other_ref, anchor_ref, momentum_ref, local_ref, *out):
        anchor_new_ref, moment_new_ref, base_ref = out
        in_own = pl.program_id(0) // 3 == s_ref[CORE]
        outer_grad = jnp.where(in_own, own_ref[...], other_ref[...]) / 4
        anchor_new, moment_new = nesterov(outer_grad, anchor_ref[...], momentum_ref[...])
        anchor_new_ref[...] = anchor_new
        moment_new_ref[...] = moment_new
        kept = mix_weight * (1.0 - inner_rate * weight_decay)
        base_ref[...] = kept * local_ref[...] + (1.0 - mix_weight) * anchor_new

    def half(array):
        return (array, (rows // 6, features), lambda i, s: (i % 3, 0))

    out = rowwise(shaped(f32, rows, features), 6)
    return order.call(
        kernel,
        [half(own), half(other)] + [rowwise(a, 6) for a in (anchor, momentum, local)],
        [out, out, out],
        (6,),
        expected["nesterov"],
    )


def final_update(order, first, fixes, p3, qa, qb, first_old, second_old, base, made=(), keys=()):
    rows, features = base.shape
    block = (rows // 6, features)
    steps = qa.shape[0] // block[0]
    scale = keys[2] if keys else None

    def kernel(s_ref, fix_ref, p_ref, a_ref, b_ref, first_ref, second_ref, base_ref, *rest):
        outs = rest[len(keys[:2]) + len(made) :]
        gradient = p_ref[...] + a_ref[...].astype(f32) + b_ref[...].astype(f32)
        first_new = beta_first * first_ref[...] + (1.0 - beta_first) * gradient
        second_new = beta_second * second_ref[...] + (1.0 - beta_second) * gradient * gradient
        root = jnp.sqrt(second_new * fix_ref[1]) + epsilon
        step = (mix_weight * inner_rate) * fix_ref[0]
        outs[0][...] = base_ref[...] - step * first_new / root
        outs[1][...] = first_new
        outs[2][...] = second_new
        if keys:
            outs[3][...] = (rest[0][...] * scale + rest[1][...].astype(f32)).astype(bf16)

    def at(array, offset):
        return (array, block, lambda i, *_: (offset + i, 0))

    out = at(shaped(f32, rows, features), first)
    inputs = [at(p3, first), rowwise(qa, steps), rowwise(qb, steps)]
    inputs += [at(a, first) for a in (first_old, second_old, base)]
    inputs += [rowwise(a, steps) for a in keys[:2]]
    aliases = {2 + len(inputs) + i: i for i in range(len(made))}
    return order.call(
        kernel,
        inputs + [(a, None, None) for a in made],
        [out] * 3 + ([rowwise(shaped(bf16, *keys[0].shape), steps)] if keys else []),
        (steps,),
        0 if keys else expected["first half"],
        aliases,
        fixes,
    )


def pair_pass(normed, key_grad, local, first_old, second_old, anchor, momentum, inner_step):
    width = normed.shape[1]
    rows = local.shape[0]
    scale = width ** (-0.5)
    me = lax.axis_index("fsdp")
    core = lax.axis_index("rep") % 2
    y, z = me % 2, me // 2
    inside = (z == 1) | (z == 2)
    far = jnp.where(z < 2, 3, 0)
    middle = jnp.where(z < 2, 2, 1)
    order = Order(jnp.stack([far, middle, z ^ 1, z, y, inside, ~inside, core]).astype(jnp.int32))

    def along(links):
        pairs = [(2 * a + c, 2 * b + c) for a, b in links for c in (0, 1)]
        return lambda value: lax.ppermute(value, "fsdp", pairs)

    outer = along([(0, 1), (1, 0), (2, 3), (3, 2)])
    inner = along([(1, 2), (2, 1)])

    def swap(value):
        return lax.ppermute(value, "fsdp", [(i, i ^ 1) for i in range(8)])

    def replica(value, bit):
        return lax.ppermute(value, "rep", [(i, i ^ bit) for i in range(4)])

    g_pair = swap(key_grad)
    weight = rounded(order, local)
    w_beside = outer(weight)
    w_inner = inner(weight)
    x0 = swap(first_piece(order, normed, rows))
    own_delta, other_delta = delta_halves(order, anchor, local)
    delta_core = replica(other_delta, 1)
    fixes = 1.0 / jnp.stack(corrections(inner_step))
    two, three, mine = split(order, normed, rows, g_pair, fixes)
    x12 = swap(two)
    delta = total_of(order, own_delta, delta_core)
    delta_there = replica(delta, 2)

    def partial(k, theirs, at, dtype, span):
        return gradient_part(order, mine, k, theirs, at, key_grad, g_pair, scale, dtype, span)

    p0 = partial(0, x0, 0, bf16, expected["first part"])
    send, across = choose_sends(order, p0, w_inner, w_beside)
    c1 = outer(send)
    w_across = inner(across)
    three, own01 = input_two(order, key_grad, g_pair, weight, w_beside, three, scale)
    x3 = swap(three)
    known = (w_beside, weight)
    own_total = key_sums(order, None, [(mine, 2), (mine, 3)], known, expected["early own"])
    total = total_of(order, delta, delta_there)
    total_there = replica(total, 1)
    p1 = partial(1, x12, 0, bf16, expected["second part"])
    p2 = partial(2, x12, 1, f32, 1)
    anchor_new, moment_new, base = nesterov_pass(
        order, total, total_there, anchor, momentum, local
    )
    pair_total = key_sums(order, None, [(x12, 1)], known[:1], expected["early pair"])

    s0a, send_a, s0b, send_b = first_handoff(order, p0, c1, p1, w_across)
    c2a, q2a = outer(send_a), inner(s0a)
    c2b, q2b = outer(send_b), inner(s0b)
    i2, own2, w_middle = input_one(
        order, key_grad, g_pair, w_inner, 0, c1, scale, expected["input middle"]
    )
    g2 = swap(i2)
    input_grad = input_join(
        order,
        (OWN, BESIDE),
        [[(own01, 0)], [(own01, 1)]],
        [[(x3, 1)], [(x3, 2)]],
        normed.shape,
        expected["join two"],
    )
    p3 = partial(3, x3, 0, f32, 0)
    i3, own3a, w_far_a = input_one(
        order, key_grad, g_pair, w_across, 0, c2a, scale, expected["input far"], [x3]
    )
    g3a = swap(i3)
    s1, t = second_handoff(order, 0, p1, c2a, p2, q2a, [x3], expected["early sums"])
    qaa, qba = outer(t), inner(s1)
    pair_total = key_sums(
        order,
        pair_total,
        [(x12, 0), (x3, 0)],
        (w_middle, weight),
        expected["pair sums"],
        before=[g2],
    )
    i3, own3b, w_far_b = input_one(
        order, key_grad, g_pair, w_across, 2, c2b, scale, expected["input last"]
    )
    g3b = swap(i3)
    w_far = (w_far_a, w_far_b)
    key_pair = swap(
        key_sums(order, pair_total, [(x0, 0), (x0, 2)], w_far, 0, scale, bf16, [q2b])
    )
    s1, t = second_handoff(order, 4, p1, c2b, p2, q2b, [g3a, g3b], expected["late sums"])
    qab, qbb = outer(t), inner(s1)
    own_total = key_sums(
        order,
        own_total,
        [(mine, 1), (mine, 0), (mine, 2)],
        (w_middle, *w_far),
        expected["own sums"],
    )
    input_grad = input_join(
        order,
        (MIDDLE, FAR),
        [[(own2, 0)], [(own3a, 0), (own3b, 0)]],
        [[(g2, 0)], [(g3a, 0), (g3b, 0)]],
        normed.shape,
        expected["join last"],
        input_grad,
    )
    state = (first_old, second_old, base)
    made = final_update(order, 0, fixes, p3, qaa, qba, *state)
    merged, first_new, second_new, keys = final_update(
        order, 4, fixes, p3, qab, qbb, *state, made, (own_total, key_pair, scale)
    )
    return (keys, input_grad, merged, first_new, second_new, anchor_new, moment_new)


def body(normed, key_grad, master, first_moment, second_moment, anchor, momentum, inner_step):
    local = master[0]
    sizes = (lax.axis_size("rep"), lax.axis_size("fsdp"))
    inner_pass = pair_pass if sizes == (4, 8) else whole_pass
    keys, input_grad, merged, first_new, second_new, anchor_new, moment_new = inner_pass(
        normed, key_grad, local, first_moment[0], second_moment[0], anchor, momentum, inner_step
    )
    return (
        keys,
        input_grad,
        merged[None],
        first_new[None],
        second_new[None],
        anchor_new,
        moment_new,
    )


def solution(mesh):
    in_specs = (
        P(("rep", "fsdp"), None),
        P(("rep", "fsdp"), None),
        P("rep", "fsdp", None),
        P("rep", "fsdp", None),
        P("rep", "fsdp", None),
        P("fsdp", None),
        P("fsdp", None),
        P(),
    )
    out_specs = (
        P(("rep", "fsdp"), None),
        P(("rep", "fsdp"), None),
        P("rep", "fsdp", None),
        P("rep", "fsdp", None),
        P("rep", "fsdp", None),
        P("fsdp", None),
        P("fsdp", None),
    )
    return jax.shard_map(body, mesh=mesh, in_specs=in_specs, out_specs=out_specs, check_vma=False)
```

profile of v0, /device:TPU:0, one launch (start us, length us, event | category | flops | bytes accessed | tf_op | source)
XLA Modules:
  0.0 122.9 jit_solution(6793765024373377309)
XLA Ops:
  0.6 3.0 %collective-permute-start = (bf16[384,1024]{1,0:T(8,128)(2,1)}, bf16[384,1024]{1,0:T(8,128)(2,1)S(1)}, u32[]{:S(2)}, u32[]{:S(2)}) collective-permute-start(bf16[384,1024]{1,0:T(8,128)(2,1)} %refs_1_.11), channel_id=1, source_target_pairs={{0,1},{1,0},{2,3},{3,2},{4,5},{5,4},{6,7},{7,6},{8,9},{9,8},{10,11... | collective-permute-start | bytes 2359304 | tf_op jit(solution)/shard_map/ppermute | solution.py:551
  6.9 4.4 %collective-permute-start.1 = (bf16[576,1024]{1,0:T(8,128)(2,1)S(1)}, bf16[576,1024]{1,0:T(8,128)(2,1)S(1)}, u32[]{:S(2)}, u32[]{:S(2)}) collective-permute-start(bf16[576,1024]{1,0:T(8,128)(2,1)S(1)} %get-tuple-element.89.refs_3_.refs_4_), channel_id=1, source_target_pairs={{0,2},{1,3},{2,0},{3,1},{4,6},{5,7},{6,4},{7,5},{8,10},{9,11},{10,... | collective-permute-start | bytes 3538952 | tf_op jit(solution)/shard_map/ppermute | solution.py:545
  11.3 2.0 %copy-done.7 = bf16[384,4608]{1,0:T(8,128)(2,1)S(1)} copy-done((bf16[384,4608]{1,0:T(8,128)(2,1)S(1)}, bf16[384,4608]{1,0:T(8,128)(2,1)}, u32[]{:S(2)}) %copy-start.7) | copy-done | bytes 3538968
  16.8 5.4 %collective-permute-done.refs_3_.refs_4_.refs_2_ = bf16[384,1024]{1,0:T(8,128)(2,1)S(1)} collective-permute-done((bf16[384,1024]{1,0:T(8,128)(2,1)}, bf16[384,1024]{1,0:T(8,128)(2,1)S(1)}, u32[]{:S(2)}, u32[]{:S(2)}) %collective-permute-start) | collective-permute-done | bytes 786464 | tf_op jit(solution)/shard_map/ppermute | solution.py:551
  22.2 2.3 %shard_map.138 = (bf16[1152,384]{1,0:T(8,128)(2,1)S(1)}, bf16[1728,384]{1,0:T(8,128)(2,1)S(1)}, bf16[2304,384]{1,0:T(8,128)(2,1)S(1)}, s32[8,128]{1,0:T(8,128)S(1)}) custom-call(s32[8]{0:T(128)S(1)} %stack.48.refs_0_, f32[2]{0:T(128)S(1)} %maximum_divide_fusion.refs_1_, bf16[384,4608]{1,0:T(8,128)(2,1)S(1)} %copy-done.8, ...), custom_call_target="tpu_custom_call" | custom-call | flops 30000001024 | tf_op jit(solution)/shard_map/pallas_call | solution.py:112
  25.3 2.1 %collective-permute-start.8 = (f32[288,1024]{1,0:T(8,128)S(1)}, f32[288,1024]{1,0:T(8,128)S(1)}, u32[]{:S(2)}, u32[]{:S(2)}) collective-permute-start(f32[288,1024]{1,0:T(8,128)S(1)} %get-tuple-element.103.refs_1_), channel_id=1, source_target_pairs={{0,16},{8,24},{16,0},{24,8},{1,17},{9,25},{17,1},{25,9},{2,18},{10... | collective-permute-start | bytes 3538952 | tf_op jit(solution)/shard_map/ppermute | solution.py:554
  28.9 2.8 %collective-permute-done.2.refs_2_.refs_1_ = bf16[576,384]{1,0:T(8,128)(2,1)S(1)} collective-permute-done((bf16[576,384]{1,0:T(8,128)(2,1)S(1)}, bf16[576,384]{1,0:T(8,128)(2,1)S(1)}, u32[]{:S(2)}, u32[]{:S(2)}) %collective-permute-start.2) | collective-permute-done | bytes 442400 | tf_op jit(solution)/shard_map/ppermute | solution.py:551
  31.7 2.3 %shard_map.140 = (bf16[576,1024]{1,0:T(8,128)(2,1)S(1)}, s32[8,128]{1,0:T(8,128)S(1)}) custom-call(s32[8]{0:T(128)S(1)} %stack.48.refs_0_, bf16[2304,384]{1,0:T(8,128)(2,1)S(1)} %get-tuple-element.88.refs_1_.refs_2_.refs_3_, bf16[576,384]{1,0:T(8,128)(2,1)S(1)} %collective-permute-done.2.refs_2_.refs_1_, bf16[384,1024]{1,0:T(8,128)(2,1)S(1)} %copy-done.3, ...), custom_call_target="tpu_custom_call" | custom-call | tf_op jit(solution)/shard_map/pallas_call | solution.py:112
  34.1 2.6 %collective-permute-done.1.refs_3_.refs_4_.refs_2_ = bf16[576,1024]{1,0:T(8,128)(2,1)S(1)} collective-permute-done((bf16[576,1024]{1,0:T(8,128)(2,1)S(1)}, bf16[576,1024]{1,0:T(8,128)(2,1)S(1)}, u32[]{:S(2)}, u32[]{:S(2)}) %collective-permute-start.1) | collective-permute-done | bytes 1179680 | tf_op jit(solution)/shard_map/ppermute | solution.py:545
  37.5 1.8 %collective-permute-start.6 = (bf16[576,1024]{1,0:T(8,128)(2,1)S(1)}, bf16[576,1024]{1,0:T(8,128)(2,1)S(1)}, u32[]{:S(2)}, u32[]{:S(2)}) collective-permute-start(bf16[576,1024]{1,0:T(8,128)(2,1)S(1)} %get-tuple-element.101), channel_id=1, source_target_pairs={{0,2},{1,3},{2,0},{3,1},{4,6},{5,7},{6,4},{7,5},{8,10},{9,11},{10,... | collective-permute-start | bytes 3538952 | tf_op jit(solution)/shard_map/ppermute | solution.py:545
  40.0 3.4 %shard_map.142 = (bf16[1728,384]{1,0:T(8,128)(2,1)S(1)}, bf16[1152,384]{1,0:T(8,128)(2,1)S(1)}, s32[8,128]{1,0:T(8,128)S(1)}) custom-call(s32[8]{0:T(128)S(1)} %stack.48.refs_0_, bf16[384,1024]{1,0:T(8,128)(2,1)S(1)} %copy-done.3, bf16[384,1024]{1,0:T(8,128)(2,1)S(1)} %collective-permute-done.refs_3_.refs_4_.refs_2_, ...), custom_call_target="tpu_custom_call", output_to_operand_aliasing={{0}: (5, {})} | custom-call | flops 12000000000 | tf_op jit(solution)/shard_map/pallas_call | solution.py:112
  44.0 2.5 %shard_map.143 = (f32[384,1024]{1,0:T(8,128)S(1)}, s32[8,128]{1,0:T(8,128)S(1)}) custom-call(s32[8]{0:T(128)S(1)} %stack.48.refs_0_, bf16[2304,384]{1,0:T(8,128)(2,1)S(1)} %get-tuple-element.88.refs_1_.refs_2_.refs_3_, bf16[2304,384]{1,0:T(8,128)(2,1)S(1)} %get-tuple-element.88.refs_1_.refs_2_.refs_3_, ...), custom_call_target="tpu_custom_call" | custom-call | tf_op jit(solution)/shard_map/pallas_call | solution.py:112
  46.5 5.2 %collective-permute-done.8.refs_2_ = f32[288,1024]{1,0:T(8,128)S(1)} collective-permute-done((f32[288,1024]{1,0:T(8,128)S(1)}, f32[288,1024]{1,0:T(8,128)S(1)}, u32[]{:S(2)}, u32[]{:S(2)}) %collective-permute-start.8) | collective-permute-done | bytes 1179680 | tf_op jit(solution)/shard_map/ppermute | solution.py:554
  52.5 2.3 %shard_map.145 = (bf16[576,1024]{1,0:T(8,128)(2,1)S(1)}, s32[8,128]{1,0:T(8,128)S(1)}) custom-call(s32[8]{0:T(128)S(1)} %stack.48.refs_0_, bf16[2304,384]{1,0:T(8,128)(2,1)S(1)} %get-tuple-element.88.refs_1_.refs_2_.refs_3_, bf16[1152,384]{1,0:T(8,128)(2,1)S(1)} %collective-permute-done.7.refs_2_.refs_1_, bf16[384,1024]{1,0:T(8,128)(2,1)S(1)} %copy-done.3, ...), custom_call_target="tpu_custom_call" | custom-call | flops 30000001024 | tf_op jit(solution)/shard_map/pallas_call | solution.py:112
  54.8 2.4 %shard_map.146 = (f32[576,1024]{1,0:T(8,128)S(1)}, s32[8,128]{1,0:T(8,128)S(1)}) custom-call(s32[8]{0:T(128)S(1)} %stack.48.refs_0_, bf16[2304,384]{1,0:T(8,128)(2,1)S(1)} %get-tuple-element.88.refs_1_.refs_2_.refs_3_, bf16[1152,384]{1,0:T(8,128)(2,1)S(1)} %collective-permute-done.7.refs_2_.refs_1_, bf16[384,1024]{1,0:T(8,128)(2,1)S(1)} %copy-done.3, ...), custom_call_target="tpu_custom_call" | custom-call | flops 1000000000 | tf_op jit(solution)/shard_map/pallas_call | solution.py:112
  57.3 3.9 %shard_map.147 = (f32[576,1024]{1,0:T(8,128)}, f32[576,1024]{1,0:T(8,128)}, f32[576,1024]{1,0:T(8,128)S(1)}, s32[8,128]{1,0:T(8,128)S(1)}) custom-call(s32[8]{0:T(128)S(1)} %stack.48.refs_0_, f32[288,1024]{1,0:T(8,128)S(1)} %get-tuple-element.109.refs_1_, f32[288,1024]{1,0:T(8,128)S(1)} %collective-permute-done.10.refs_2_, f32[576,1024]{1,0:T(8,128)S(1)} %copy-done, ...), custom_call_target="tpu_custom_call" | custom-call | flops 1000000000 | tf_op jit(solution)/shard_map/pallas_call | solution.py:112
  61.2 1.8 %shard_map.148 = (f32[384,1024]{1,0:T(8,128)S(1)}, s32[8,128]{1,0:T(8,128)S(1)}) custom-call(s32[8]{0:T(128)S(1)} %stack.48.refs_0_, bf16[1152,384]{1,0:T(8,128)(2,1)S(1)} %collective-permute-done.7.refs_2_.refs_1_, bf16[576,1024]{1,0:T(8,128)(2,1)S(1)} %collective-permute-done.1.refs_3_.refs_4_.refs_2_, s32[8,128]{1,0:T(8,128)S(1)} %get-tuple-element.112.refs_3_), custom_call_target="tpu_custom_call" | custom-call | tf_op jit(solution)/shard_map/pallas_call | solution.py:112
  65.4 3.7 %collective-permute-start.13 = (bf16[384,1024]{1,0:T(8,128)(2,1)S(1)}, bf16[384,1024]{1,0:T(8,128)(2,1)S(1)}, u32[]{:S(2)}, u32[]{:S(2)}) collective-permute-start(bf16[384,1024]{1,0:T(8,128)(2,1)S(1)} %get-tuple-element.121), channel_id=1, source_target_pairs={{0,2},{1,3},{2,0},{3,1},{4,6},{5,7},{6,4},{7,5},{8,10},{9,11},{10,... | collective-permute-start | bytes 2359304 | tf_op jit(solution)/shard_map/ppermute | solution.py:545
  69.8 2.0 %shard_map.150 = (bf16[576,384]{1,0:T(8,128)(2,1)S(1)}, bf16[576,384]{1,0:T(8,128)(2,1)S(1)}, bf16[576,1024]{1,0:T(8,128)(2,1)S(1)}, s32[8,128]{1,0:T(8,128)S(1)}) custom-call(s32[8]{0:T(128)S(1)} %stack.48.refs_0_, bf16[384,1024]{1,0:T(8,128)(2,1)S(1)} %copy-done.3, bf16[384,1024]{1,0:T(8,128)(2,1)S(1)} %collective-permute-done.refs_3_.refs_4_.refs_2_, ...), custom_call_target="tpu_custom_call" | custom-call | tf_op jit(solution)/shard_map/pallas_call | solution.py:112
  72.4 2.1 %collective-permute-start.11 = (bf16[192,1024]{1,0:T(8,128)(2,1)S(1)}, bf16[192,1024]{1,0:T(8,128)(2,1)S(1)}, u32[]{:S(2)}, u32[]{:S(2)}) collective-permute-start(bf16[192,1024]{1,0:T(8,128)(2,1)S(1)} %get-tuple-element.118), channel_id=1, source_target_pairs={{0,2},{1,3},{2,0},{3,1},{4,6},{5,7},{6,4},{7,5},{8,10},{9,11},{10,... | collective-permute-start | bytes 1179656 | tf_op jit(solution)/shard_map/ppermute | solution.py:545
  74.5 4.7 %collective-permute-done.5.refs_3_.refs_4_.refs_2_.refs_5_ = bf16[1728,384]{1,0:T(8,128)(2,1)S(1)} collective-permute-done((bf16[1728,384]{1,0:T(8,128)(2,1)S(1)}, bf16[1728,384]{1,0:T(8,128)(2,1)S(1)}, u32[]{:S(2)}, u32[]{:S(2)}) %collective-permute-start.5) | collective-permute-done | bytes 1327136 | tf_op jit(solution)/shard_map/ppermute | solution.py:551
  79.8 4.1 %shard_map.151 = (bf16[384,4608]{1,0:T(8,128)(2,1)}, s32[8,128]{1,0:T(8,128)S(1)}) custom-call(s32[8]{0:T(128)S(1)} %stack.48.refs_0_, bf16[1152,384]{1,0:T(8,128)(2,1)S(1)} %get-tuple-element.100.refs_1_.refs_2_, bf16[1152,384]{1,0:T(8,128)(2,1)S(1)} %get-tuple-element.100.refs_1_.refs_2_, ...), custom_call_target="tpu_custom_call" | custom-call | tf_op jit(solution)/shard_map/pallas_call | solution.py:112
  83.9 2.4 %shard_map.152 = (f32[576,1024]{1,0:T(8,128)S(1)}, s32[8,128]{1,0:T(8,128)S(1)}) custom-call(s32[8]{0:T(128)S(1)} %stack.48.refs_0_, bf16[2304,384]{1,0:T(8,128)(2,1)S(1)} %get-tuple-element.88.refs_1_.refs_2_.refs_3_, bf16[1728,384]{1,0:T(8,128)(2,1)S(1)} %collective-permute-done.5.refs_3_.refs_4_.refs_2_.refs_5_, bf16[384,1024]{1,0:T(8,128)(2,1)S(1)} %copy-done.3, ...), custom_call_target="tpu_custom_call" | custom-call | tf_op jit(solution)/shard_map/pallas_call | solution.py:112
  90.9 4.4 %collective-permute-start.21 = (bf16[384,1024]{1,0:T(8,128)(2,1)S(1)}, bf16[384,1024]{1,0:T(8,128)(2,1)S(1)}, u32[]{:S(2)}, u32[]{:S(2)}) collective-permute-start(bf16[384,1024]{1,0:T(8,128)(2,1)S(1)} %get-tuple-element.144), channel_id=1, source_target_pairs={{0,2},{1,3},{2,0},{3,1},{4,6},{5,7},{6,4},{7,5},{8,10},{9,11},{10,... | collective-permute-start | bytes 2359304 | tf_op jit(solution)/shard_map/ppermute | solution.py:545
  96.2 2.6 %shard_map.155 = (f32[384,1024]{1,0:T(8,128)S(1)}, s32[8,128]{1,0:T(8,128)S(1)}) custom-call(s32[8]{0:T(128)S(1)} %stack.48.refs_0_, bf16[1152,384]{1,0:T(8,128)(2,1)S(1)} %collective-permute-done.7.refs_2_.refs_1_, bf16[1728,384]{1,0:T(8,128)(2,1)S(1)} %collective-permute-done.5.refs_3_.refs_4_.refs_2_.refs_5_, ...), custom_call_target="tpu_custom_call" | custom-call | tf_op jit(solution)/shard_map/pallas_call | solution.py:112
  100.6 1.8 %shard_map.157 = (bf16[384,1024]{1,0:T(8,128)(2,1)S(1)}, s32[8,128]{1,0:T(8,128)S(1)}) custom-call(s32[8]{0:T(128)S(1)} %stack.48.refs_0_, bf16[576,384]{1,0:T(8,128)(2,1)S(1)} %collective-permute-done.2.refs_2_.refs_1_, bf16[576,384]{1,0:T(8,128)(2,1)S(1)} %collective-permute-done.2.refs_2_.refs_1_, ...), custom_call_target="tpu_custom_call" | custom-call | tf_op jit(solution)/shard_map/pallas_call | solution.py:112
  104.1 2.8 %collective-permute-done.17.refs_6_ = bf16[192,384]{1,0:T(8,128)(2,1)S(1)} collective-permute-done((bf16[192,384]{1,0:T(8,128)(2,1)S(1)}, bf16[192,384]{1,0:T(8,128)(2,1)S(1)}, u32[]{:S(2)}, u32[]{:S(2)}) %collective-permute-start.17) | collective-permute-done | bytes 147488 | tf_op jit(solution)/shard_map/ppermute | solution.py:551
  107.7 1.7 %collective-permute-start.18 = (bf16[192,1024]{1,0:T(8,128)(2,1)S(1)}, bf16[192,1024]{1,0:T(8,128)(2,1)S(1)}, u32[]{:S(2)}, u32[]{:S(2)}) collective-permute-start(bf16[192,1024]{1,0:T(8,128)(2,1)S(1)} %get-tuple-element.137), channel_id=1, source_target_pairs={{0,2},{1,3},{2,0},{3,1},{4,6},{5,7},{6,4},{7,5},{8,10},{9,11},{10,... | collective-permute-start | bytes 1179656 | tf_op jit(solution)/shard_map/ppermute | solution.py:545
  110.1 2.6 %shard_map.159 = (f32[384,1024]{1,0:T(8,128)S(1)}, s32[8,128]{1,0:T(8,128)S(1)}) custom-call(s32[8]{0:T(128)S(1)} %stack.48.refs_0_, bf16[2304,384]{1,0:T(8,128)(2,1)S(1)} %get-tuple-element.88.refs_1_.refs_2_.refs_3_, bf16[2304,384]{1,0:T(8,128)(2,1)S(1)} %get-tuple-element.88.refs_1_.refs_2_.refs_3_, ...), custom_call_target="tpu_custom_call" | custom-call | tf_op jit(solution)/shard_map/pallas_call | solution.py:112
  112.7 4.1 %shard_map.160 = (bf16[384,4608]{1,0:T(8,128)(2,1)}, s32[8,128]{1,0:T(8,128)S(1)}) custom-call(s32[8]{0:T(128)S(1)} %stack.48.refs_0_, bf16[576,384]{1,0:T(8,128)(2,1)S(1)} %get-tuple-element.146.refs_1_, bf16[384,384]{1,0:T(8,128)(2,1)S(1)} %get-tuple-element.147.refs_2_, ...), custom_call_target="tpu_custom_call", output_to_operand_aliasing={{0}: (7, {})} | custom-call | tf_op jit(solution)/shard_map/pallas_call | solution.py:112
  116.8 3.4 %shard_map.161 = (f32[576,1024]{1,0:T(8,128)}, f32[576,1024]{1,0:T(8,128)}, f32[576,1024]{1,0:T(8,128)}, s32[8,128]{1,0:T(8,128)S(1)}) custom-call(s32[8]{0:T(128)S(1)} %stack.48.refs_0_, f32[2]{0:T(128)S(1)} %maximum_divide_fusion.refs_1_, f32[576,1024]{1,0:T(8,128)S(1)} %get-tuple-element.117.refs_2_, ...), custom_call_target="tpu_custom_call" | custom-call | flops 12000000000 | tf_op jit(solution)/shard_map/pallas_call | solution.py:112
  120.3 2.6 %shard_map.162 = (f32[576,1024]{1,0:T(8,128)}, f32[576,1024]{1,0:T(8,128)}, f32[576,1024]{1,0:T(8,128)}, bf16[384,1024]{1,0:T(8,128)(2,1)}, s32[8,128]{1,0:T(8,128)}) custom-call(s32[8]{0:T(128)S(1)} %stack.48.refs_0_, f32[2]{0:T(128)S(1)} %maximum_divide_fusion.refs_1_, ...), custom_call_target="tpu_custom_call", output_to_operand_aliasing={{0}: (10, {}), {1}: (11, {}), {2}: (12, {})} | custom-call | tf_op jit(solution)/shard_map/pallas_call | solution.py:112
  (62 shorter events, 25.8 us)
Async XLA Ops:
  0.6 21.6 %collective-permute-start = (bf16[384,1024]{1,0:T(8,128)(2,1)}, bf16[384,1024]{1,0:T(8,128)(2,1)S(1)}, u32[]{:S(2)}, u32[]{:S(2)}) collective-permute-start(bf16[384,1024]{1,0:T(8,128)(2,1)} %refs_1_.11), channel_id=1, source_target_pairs={{0,1},{1,0},{2,3},{3,2},{4,5},{5,4},{6,7},{7,6},{8,9},{9,8},{10,11... | collective-permute-start | bytes 2359304 | tf_op jit(solution)/shard_map/ppermute | solution.py:551
  3.7 1.7 %copy-start.1 = (f32[1,576,1024]{2,1,0:T(8,128)S(1)}, f32[1,576,1024]{2,1,0:T(8,128)}, u32[]{:S(2)}) copy-start(f32[1,576,1024]{2,1,0:T(8,128)} %param.10) | copy-start | bytes 7077892
  5.4 9.3 %copy-start.2 = (f32[1,576,1024]{2,1,0:T(8,128)S(1)}, f32[1,576,1024]{2,1,0:T(8,128)}, u32[]{:S(2)}) copy-start(f32[1,576,1024]{2,1,0:T(8,128)} %param.10) | copy-start | bytes 7077892
  6.1 27.9 %collective-permute-start.4 = (bf16[576,1024]{1,0:T(8,128)(2,1)S(1)}, bf16[576,1024]{1,0:T(8,128)(2,1)S(1)}, u32[]{:S(2)}, u32[]{:S(2)}) collective-permute-start(bf16[576,1024]{1,0:T(8,128)(2,1)S(1)} %get-tuple-element.89.refs_3_.refs_4_), channel_id=1, source_target_pairs={{2,4},{3,5},{4,2},{5,3},{10,12},{11,13},{12,10},{13,11},{18,20},{1... | collective-permute-start | bytes 3538952 | tf_op jit(solution)/shard_map/ppermute | solution.py:545
  6.9 29.8 %collective-permute-start.1 = (bf16[576,1024]{1,0:T(8,128)(2,1)S(1)}, bf16[576,1024]{1,0:T(8,128)(2,1)S(1)}, u32[]{:S(2)}, u32[]{:S(2)}) collective-permute-start(bf16[576,1024]{1,0:T(8,128)(2,1)S(1)} %get-tuple-element.89.refs_3_.refs_4_), channel_id=1, source_target_pairs={{0,2},{1,3},{2,0},{3,1},{4,6},{5,7},{6,4},{7,5},{8,10},{9,11},{10,... | collective-permute-start | bytes 3538952 | tf_op jit(solution)/shard_map/ppermute | solution.py:545
  11.3 2.0 %copy-start.7 = (bf16[384,4608]{1,0:T(8,128)(2,1)S(1)}, bf16[384,4608]{1,0:T(8,128)(2,1)}, u32[]{:S(2)}) copy-start(bf16[384,4608]{1,0:T(8,128)(2,1)} %refs_2_.1) | copy-start | bytes 10616836
  13.3 1.7 %copy-start = (f32[576,1024]{1,0:T(8,128)S(1)}, f32[576,1024]{1,0:T(8,128)}, u32[]{:S(2)}) copy-start(f32[576,1024]{1,0:T(8,128)} %refs_3_.10) | copy-start | bytes 7077892
  14.1 17.6 %collective-permute-start.2 = (bf16[576,384]{1,0:T(8,128)(2,1)S(1)}, bf16[576,384]{1,0:T(8,128)(2,1)S(1)}, u32[]{:S(2)}, u32[]{:S(2)}) collective-permute-start(bf16[576,384]{1,0:T(8,128)(2,1)S(1)} %get-tuple-element.91), channel_id=1, source_target_pairs={{0,1},{1,0},{2,3},{3,2},{4,5},{5,4},{6,7},{7,6},{8,9},{9,8},{10,11... | collective-permute-start | bytes 1327112 | tf_op jit(solution)/shard_map/ppermute | solution.py:551
  14.9 7.3 %copy-start.8 = (bf16[384,4608]{1,0:T(8,128)(2,1)S(1)}, bf16[384,4608]{1,0:T(8,128)(2,1)}, u32[]{:S(2)}) copy-start(bf16[384,4608]{1,0:T(8,128)(2,1)} %refs_2_.1) | copy-start | bytes 10616836
  15.8 8.7 %collective-permute-start.3 = (f32[288,1024]{1,0:T(8,128)S(1)}, f32[288,1024]{1,0:T(8,128)S(1)}, u32[]{:S(2)}, u32[]{:S(2)}) collective-permute-start(f32[288,1024]{1,0:T(8,128)S(1)} %get-tuple-element.93), channel_id=1, source_target_pairs={{0,8},{8,0},{16,24},{24,16},{1,9},{9,1},{17,25},{25,17},{2,10},{10... | collective-permute-start | bytes 3538952 | tf_op jit(solution)/shard_map/ppermute | solution.py:554
  24.5 7.2 %copy-start.3 = (bf16[384,1024]{1,0:T(8,128)(2,1)S(1)}, bf16[384,1024]{1,0:T(8,128)(2,1)}, u32[]{:S(2)}) copy-start(bf16[384,1024]{1,0:T(8,128)(2,1)} %refs_1_.11) | copy-start | bytes 2359300
  25.3 26.4 %collective-permute-start.8 = (f32[288,1024]{1,0:T(8,128)S(1)}, f32[288,1024]{1,0:T(8,128)S(1)}, u32[]{:S(2)}, u32[]{:S(2)}) collective-permute-start(f32[288,1024]{1,0:T(8,128)S(1)} %get-tuple-element.103.refs_1_), channel_id=1, source_target_pairs={{0,16},{8,24},{16,0},{24,8},{1,17},{9,25},{17,1},{25,9},{2,18},{10... | collective-permute-start | bytes 3538952 | tf_op jit(solution)/shard_map/ppermute | solution.py:554
  27.4 25.1 %collective-permute-start.7 = (bf16[1152,384]{1,0:T(8,128)(2,1)S(1)}, bf16[1152,384]{1,0:T(8,128)(2,1)S(1)}, u32[]{:S(2)}, u32[]{:S(2)}) collective-permute-start(bf16[1152,384]{1,0:T(8,128)(2,1)S(1)} %get-tuple-element.102), channel_id=1, source_target_pairs={{0,1},{1,0},{2,3},{3,2},{4,5},{5,4},{6,7},{7,6},{8,9},{9,8},{10,11... | collective-permute-start | bytes 2654216 | tf_op jit(solution)/shard_map/ppermute | solution.py:551
  37.5 26.6 %collective-permute-start.6 = (bf16[576,1024]{1,0:T(8,128)(2,1)S(1)}, bf16[576,1024]{1,0:T(8,128)(2,1)S(1)}, u32[]{:S(2)}, u32[]{:S(2)}) collective-permute-start(bf16[576,1024]{1,0:T(8,128)(2,1)S(1)} %get-tuple-element.101), channel_id=1, source_target_pairs={{0,2},{1,3},{2,0},{3,1},{4,6},{5,7},{6,4},{7,5},{8,10},{9,11},{10,... | collective-permute-start | bytes 3538952 | tf_op jit(solution)/shard_map/ppermute | solution.py:545
  39.3 24.8 %collective-permute-start.9 = (bf16[576,1024]{1,0:T(8,128)(2,1)S(1)}, bf16[576,1024]{1,0:T(8,128)(2,1)S(1)}, u32[]{:S(2)}, u32[]{:S(2)}) collective-permute-start(bf16[576,1024]{1,0:T(8,128)(2,1)S(1)} %get-tuple-element.108), channel_id=1, source_target_pairs={{2,4},{3,5},{4,2},{5,3},{10,12},{11,13},{12,10},{13,11},{18,20},{1... | collective-permute-start | bytes 3538952 | tf_op jit(solution)/shard_map/ppermute | solution.py:545
  43.4 35.7 %collective-permute-start.5 = (bf16[1728,384]{1,0:T(8,128)(2,1)S(1)}, bf16[1728,384]{1,0:T(8,128)(2,1)S(1)}, u32[]{:S(2)}, u32[]{:S(2)}) collective-permute-start(bf16[1728,384]{1,0:T(8,128)(2,1)S(1)} %get-tuple-element.99), channel_id=1, source_target_pairs={{0,1},{1,0},{2,3},{3,2},{4,5},{5,4},{6,7},{7,6},{8,9},{9,8},{10,11... | collective-permute-start | bytes 3981320 | tf_op jit(solution)/shard_map/ppermute | solution.py:551
  52.4 4.8 %collective-permute-start.10 = (f32[288,1024]{1,0:T(8,128)S(1)}, f32[288,1024]{1,0:T(8,128)S(1)}, u32[]{:S(2)}, u32[]{:S(2)}) collective-permute-start(f32[288,1024]{1,0:T(8,128)S(1)} %get-tuple-element.109.refs_1_), channel_id=1, source_target_pairs={{0,8},{8,0},{16,24},{24,16},{1,9},{9,1},{17,25},{25,17},{2,10},{10... | collective-permute-start | bytes 3538952 | tf_op jit(solution)/shard_map/ppermute | solution.py:554
  54.8 2.4 %copy-start.4 = (f32[576,1024]{1,0:T(8,128)S(1)}, f32[576,1024]{1,0:T(8,128)}, u32[]{:S(2)}) copy-start(f32[576,1024]{1,0:T(8,128)} %refs_4_.1) | copy-start | bytes 7077892
  65.4 22.1 %collective-permute-start.13 = (bf16[384,1024]{1,0:T(8,128)(2,1)S(1)}, bf16[384,1024]{1,0:T(8,128)(2,1)S(1)}, u32[]{:S(2)}, u32[]{:S(2)}) collective-permute-start(bf16[384,1024]{1,0:T(8,128)(2,1)S(1)} %get-tuple-element.121), channel_id=1, source_target_pairs={{0,2},{1,3},{2,0},{3,1},{4,6},{5,7},{6,4},{7,5},{8,10},{9,11},{10,... | collective-permute-start | bytes 2359304 | tf_op jit(solution)/shard_map/ppermute | solution.py:545
  69.1 20.9 %collective-permute-start.16 = (bf16[384,1024]{1,0:T(8,128)(2,1)S(1)}, bf16[384,1024]{1,0:T(8,128)(2,1)S(1)}, u32[]{:S(2)}, u32[]{:S(2)}) collective-permute-start(bf16[384,1024]{1,0:T(8,128)(2,1)S(1)} %get-tuple-element.127), channel_id=1, source_target_pairs={{2,4},{3,5},{4,2},{5,3},{10,12},{11,13},{12,10},{13,11},{18,20},{1... | collective-permute-start | bytes 2359304 | tf_op jit(solution)/shard_map/ppermute | solution.py:545
  71.8 23.6 %collective-permute-start.15 = (bf16[576,384]{1,0:T(8,128)(2,1)S(1)}, bf16[576,384]{1,0:T(8,128)(2,1)S(1)}, u32[]{:S(2)}, u32[]{:S(2)}) collective-permute-start(bf16[576,384]{1,0:T(8,128)(2,1)S(1)} %get-tuple-element.126), channel_id=1, source_target_pairs={{0,1},{1,0},{2,3},{3,2},{4,5},{5,4},{6,7},{7,6},{8,9},{9,8},{10,11... | collective-permute-start | bytes 1327112 | tf_op jit(solution)/shard_map/ppermute | solution.py:551
  72.4 26.5 %collective-permute-start.11 = (bf16[192,1024]{1,0:T(8,128)(2,1)S(1)}, bf16[192,1024]{1,0:T(8,128)(2,1)S(1)}, u32[]{:S(2)}, u32[]{:S(2)}) collective-permute-start(bf16[192,1024]{1,0:T(8,128)(2,1)S(1)} %get-tuple-element.118), channel_id=1, source_target_pairs={{0,2},{1,3},{2,0},{3,1},{4,6},{5,7},{6,4},{7,5},{8,10},{9,11},{10,... | collective-permute-start | bytes 1179656 | tf_op jit(solution)/shard_map/ppermute | solution.py:545
  79.1 21.5 %collective-permute-start.12 = (bf16[192,1024]{1,0:T(8,128)(2,1)S(1)}, bf16[192,1024]{1,0:T(8,128)(2,1)S(1)}, u32[]{:S(2)}, u32[]{:S(2)}) collective-permute-start(bf16[192,1024]{1,0:T(8,128)(2,1)S(1)} %get-tuple-element.120), channel_id=1, source_target_pairs={{2,4},{3,5},{4,2},{5,3},{10,12},{11,13},{12,10},{13,11},{18,20},{1... | collective-permute-start | bytes 1179656 | tf_op jit(solution)/shard_map/ppermute | solution.py:545
  89.1 17.8 %collective-permute-start.14 = (bf16[384,384]{1,0:T(8,128)(2,1)S(1)}, bf16[384,384]{1,0:T(8,128)(2,1)S(1)}, u32[]{:S(2)}, u32[]{:S(2)}) collective-permute-start(bf16[384,384]{1,0:T(8,128)(2,1)S(1)} %get-tuple-element.123), channel_id=1, source_target_pairs={{0,1},{1,0},{2,3},{3,2},{4,5},{5,4},{6,7},{7,6},{8,9},{9,8},{10,11... | collective-permute-start | bytes 884744 | tf_op jit(solution)/shard_map/ppermute | solution.py:551
  90.9 25.9 %collective-permute-start.21 = (bf16[384,1024]{1,0:T(8,128)(2,1)S(1)}, bf16[384,1024]{1,0:T(8,128)(2,1)S(1)}, u32[]{:S(2)}, u32[]{:S(2)}) collective-permute-start(bf16[384,1024]{1,0:T(8,128)(2,1)S(1)} %get-tuple-element.144), channel_id=1, source_target_pairs={{0,2},{1,3},{2,0},{3,1},{4,6},{5,7},{6,4},{7,5},{8,10},{9,11},{10,... | collective-permute-start | bytes 2359304 | tf_op jit(solution)/shard_map/ppermute | solution.py:545
  95.3 21.5 %collective-permute-start.22 = (bf16[384,1024]{1,0:T(8,128)(2,1)S(1)}, bf16[384,1024]{1,0:T(8,128)(2,1)S(1)}, u32[]{:S(2)}, u32[]{:S(2)}) collective-permute-start(bf16[384,1024]{1,0:T(8,128)(2,1)S(1)} %get-tuple-element.145), channel_id=1, source_target_pairs={{2,4},{3,5},{4,2},{5,3},{10,12},{11,13},{12,10},{13,11},{18,20},{1... | collective-permute-start | bytes 2359304 | tf_op jit(solution)/shard_map/ppermute | solution.py:545
  100.1 6.8 %collective-permute-start.17 = (bf16[192,384]{1,0:T(8,128)(2,1)S(1)}, bf16[192,384]{1,0:T(8,128)(2,1)S(1)}, u32[]{:S(2)}, u32[]{:S(2)}) collective-permute-start(bf16[192,384]{1,0:T(8,128)(2,1)S(1)} %get-tuple-element.131), channel_id=1, source_target_pairs={{0,1},{1,0},{2,3},{3,2},{4,5},{5,4},{6,7},{7,6},{8,9},{9,8},{10,11... | collective-permute-start | bytes 442376 | tf_op jit(solution)/shard_map/ppermute | solution.py:551
  102.5 17.8 %collective-permute-start.20 = (bf16[384,1024]{1,0:T(8,128)(2,1)S(1)}, bf16[384,1024]{1,0:T(8,128)(2,1)S(1)}, u32[]{:S(2)}, u32[]{:S(2)}) collective-permute-start(bf16[384,1024]{1,0:T(8,128)(2,1)S(1)} %get-tuple-element.143), channel_id=1, source_target_pairs={{0,1},{1,0},{2,3},{3,2},{4,5},{5,4},{6,7},{7,6},{8,9},{9,8},{10,11... | collective-permute-start | bytes 2359304 | tf_op jit(solution)/shard_map/ppermute | solution.py:551
  107.7 12.5 %collective-permute-start.18 = (bf16[192,1024]{1,0:T(8,128)(2,1)S(1)}, bf16[192,1024]{1,0:T(8,128)(2,1)S(1)}, u32[]{:S(2)}, u32[]{:S(2)}) collective-permute-start(bf16[192,1024]{1,0:T(8,128)(2,1)S(1)} %get-tuple-element.137), channel_id=1, source_target_pairs={{0,2},{1,3},{2,0},{3,1},{4,6},{5,7},{6,4},{7,5},{8,10},{9,11},{10,... | collective-permute-start | bytes 1179656 | tf_op jit(solution)/shard_map/ppermute | solution.py:545
  109.4 10.8 %collective-permute-start.19 = (bf16[192,1024]{1,0:T(8,128)(2,1)S(1)}, bf16[192,1024]{1,0:T(8,128)(2,1)S(1)}, u32[]{:S(2)}, u32[]{:S(2)}) collective-permute-start(bf16[192,1024]{1,0:T(8,128)(2,1)S(1)} %get-tuple-element.138), channel_id=1, source_target_pairs={{2,4},{3,5},{4,2},{5,3},{10,12},{11,13},{12,10},{13,11},{18,20},{1... | collective-permute-start | bytes 1179656 | tf_op jit(solution)/shard_map/ppermute | solution.py:545
  112.7 4.1 %copy-start.5 = (f32[1,576,1024]{2,1,0:T(8,128)S(1)}, f32[1,576,1024]{2,1,0:T(8,128)}, u32[]{:S(2)}) copy-start(f32[1,576,1024]{2,1,0:T(8,128)} %param.11) | copy-start | bytes 7077892
  112.7 4.1 %copy-start.6 = (f32[1,576,1024]{2,1,0:T(8,128)S(1)}, f32[1,576,1024]{2,1,0:T(8,128)}, u32[]{:S(2)}) copy-start(f32[1,576,1024]{2,1,0:T(8,128)} %param.12) | copy-start | bytes 7077892
where the time goes:
time: 123 us
  Pallas kernels  56.8 us (46%)
  starting transfers between devices  34.1 us (28%)
  waiting for transfers between devices  26.1 us (21%)
  local copies, waits for them, and re-layouts  4.04 us (3%)
  between operations  1.85 us (2%)
    pallas_call x28, Pallas kernels, call(): pl.pallas_call(wrapped, out_shape=shapes, grid_spec=pltpu.PrefetchScalarG...  56.8 us
    ppermute x12, starting transfers between devices, along(): return lambda value: lax.ppermute(value, 'fsdp', pairs)  22.6 us
    ppermute x8, waiting for transfers between devices, swap(): return lax.ppermute(value, 'fsdp', [(i, i ^ 1) for i in range(8)])  15.8 us
    ppermute x8, starting transfers between devices, swap(): return lax.ppermute(value, 'fsdp', [(i, i ^ 1) for i in range(8)])  9.26 us
    ppermute x3, waiting for transfers between devices, replica(): return lax.ppermute(value, 'rep', [(i, i ^ bit) for i in range(4)])  5.22 us
    ppermute x12, waiting for transfers between devices, along(): return lambda value: lax.ppermute(value, 'fsdp', pairs)  5.05 us
    unnamed x18, local copies, waits for them, and re-layouts  3.95 us
  transfers between devices with their start and end apart: 23, of which 9 were waited for; matrix products, arithmetic and copies ran while one was open for 0% of the time, Pallas kernels for 44%

commit v1 on v0

--- a/solution.py
+++ b/solution.py
@@ -584,7 +584,6 @@
     anchor_new, moment_new, base = nesterov_pass(
         order, total, total_there, anchor, momentum, local
     )
-    pair_total = key_sums(order, None, [(x12, 1)], known[:1], expected["early pair"])
 
     s0a, send_a, s0b, send_b = first_handoff(order, p0, c1, p1, w_across)
     c2a, q2a = outer(send_a), inner(s0a)
@@ -593,6 +592,10 @@
         order, key_grad, g_pair, w_inner, 0, c1, scale, expected["input middle"]
     )
     g2 = swap(i2)
+    pair_total = key_sums(
+        order, None, [(x12, 0), (x12, 1)], (w_middle, w_beside), expected["early pair"]
+    )
+    own_total = key_sums(order, own_total, [(mine, 1)], (w_middle,), expected["early pair"])
     input_grad = input_join(
         order,
         (OWN, BESIDE),
@@ -601,7 +604,6 @@
         normed.shape,
         expected["join two"],
     )
-    p3 = partial(3, x3, 0, f32, 0)
     i3, own3a, w_far_a = input_one(
         order, key_grad, g_pair, w_across, 0, c2a, scale, expected["input far"], [x3]
     )
@@ -611,8 +613,8 @@
     pair_total = key_sums(
         order,
         pair_total,
-        [(x12, 0), (x3, 0)],
-        (w_middle, weight),
+        [(x3, 0)],
+        (weight,),
         expected["pair sums"],
         before=[g2],
     )
@@ -626,11 +628,12 @@
     )
     s1, t = second_handoff(order, 4, p1, c2b, p2, q2b, [g3a, g3b], expected["late sums"])
     qab, qbb = outer(t), inner(s1)
+    p3 = partial(3, x3, 0, f32, 0)
     own_total = key_sums(
         order,
         own_total,
-        [(mine, 1), (mine, 0), (mine, 2)],
-        (w_middle, *w_far),
+        [(mine, 0), (mine, 2)],
+        w_far,
         expected["own sums"],
     )
     input_grad = input_join(

time: 123 us -> 122 us (level)
  starting transfers between devices: 34.1 us -> 31.8 us
    ppermute x8, waiting for transfers between devices: 15.8 us -> 11.5 us  [swap(): return lax.ppermute(value, 'fsdp', [(i, i ^ 1) for i in range(8)])]
    ppermute x12, waiting for transfers between devices: 5.05 us -> 9.23 us  [along(): return lambda value: lax.ppermute(value, 'fsdp', pairs)]
    ppermute x12, starting transfers between devices: 22.6 us -> 20.5 us  [along(): return lambda value: lax.ppermute(value, 'fsdp', pairs)]
    pallas_call x28 -> x29, Pallas kernels: 56.8 us -> 58 us  [call(): pl.pallas_call(wrapped, out_shape=shapes, grid_spec=pltpu.PrefetchScalarG...]
  transfers between devices with their start and end apart: 23 -> 23, of which waited for: 9 -> 8; matrix products, arithmetic and copies ran while one was open for 0% -> 0% of each run, Pallas kernels for 44% -> 45%
where the time goes in v1:
time: 122 us
  Pallas kernels  58 us (48%)
  starting transfers between devices  31.8 us (26%)
  waiting for transfers between devices  25.9 us (21%)
  local copies, waits for them, and re-layouts  4.04 us (3%)
  between operations  1.87 us (2%)
    pallas_call x29, Pallas kernels, call(): pl.pallas_call(wrapped, out_shape=shapes, grid_spec=pltpu.PrefetchScalarG...  58 us
    ppermute x12, starting transfers between devices, along(): return lambda value: lax.ppermute(value, 'fsdp', pairs)  20.5 us
    ppermute x8, waiting for transfers between devices, swap(): return lax.ppermute(value, 'fsdp', [(i, i ^ 1) for i in range(8)])  11.5 us
    ppermute x12, waiting for transfers between devices, along(): return lambda value: lax.ppermute(value, 'fsdp', pairs)  9.23 us
    ppermute x8, starting transfers between devices, swap(): return lax.ppermute(value, 'fsdp', [(i, i ^ 1) for i in range(8)])  8.99 us
    ppermute x3, waiting for transfers between devices, replica(): return lax.ppermute(value, 'rep', [(i, i ^ bit) for i in range(4)])  5.22 us
    unnamed x18, local copies, waits for them, and re-layouts  3.95 us
  transfers between devices with their start and end apart: 23, of which 8 were waited for; matrix products, arithmetic and copies ran while one was open for 0% of the time, Pallas kernels for 45%

profile of v1, /device:TPU:0, one launch (start us, length us, event | category | flops | bytes accessed | tf_op | source)
XLA Modules:
  0.0 121.7 jit_solution(4888428309165597581)
XLA Ops:
  0.6 3.0 %collective-permute-start = (bf16[384,1024]{1,0:T(8,128)(2,1)}, bf16[384,1024]{1,0:T(8,128)(2,1)S(1)}, u32[]{:S(2)}, u32[]{:S(2)}) collective-permute-start(bf16[384,1024]{1,0:T(8,128)(2,1)} %refs_3_.11), channel_id=1, source_target_pairs={{0,1},{1,0},{2,3},{3,2},{4,5},{5,4},{6,7},{7,6},{8,9},{9,8},{10,11... | collective-permute-start | bytes 2359304 | tf_op jit(solution)/shard_map/ppermute | solution.py:551
  6.9 4.4 %collective-permute-start.1 = (bf16[576,1024]{1,0:T(8,128)(2,1)S(1)}, bf16[576,1024]{1,0:T(8,128)(2,1)S(1)}, u32[]{:S(2)}, u32[]{:S(2)}) collective-permute-start(bf16[576,1024]{1,0:T(8,128)(2,1)S(1)} %get-tuple-element.91.refs_3_.refs_4_.refs_2_), channel_id=1, source_target_pairs={{0,2},{1,3},{2,0},{3,1},{4,6},{5,7},{6,4},{7,5},{8,10},{9,11},{10,... | collective-permute-start | bytes 3538952 | tf_op jit(solution)/shard_map/ppermute | solution.py:545
  11.3 2.0 %copy-done.7 = bf16[384,4608]{1,0:T(8,128)(2,1)S(1)} copy-done((bf16[384,4608]{1,0:T(8,128)(2,1)S(1)}, bf16[384,4608]{1,0:T(8,128)(2,1)}, u32[]{:S(2)}) %copy-start.7) | copy-done | bytes 3538968
  16.8 5.4 %collective-permute-done.refs_3_.refs_4_.refs_2_ = bf16[384,1024]{1,0:T(8,128)(2,1)S(1)} collective-permute-done((bf16[384,1024]{1,0:T(8,128)(2,1)}, bf16[384,1024]{1,0:T(8,128)(2,1)S(1)}, u32[]{:S(2)}, u32[]{:S(2)}) %collective-permute-start) | collective-permute-done | bytes 786464 | tf_op jit(solution)/shard_map/ppermute | solution.py:551
  22.2 2.3 %shard_map.138 = (bf16[1152,384]{1,0:T(8,128)(2,1)S(1)}, bf16[1728,384]{1,0:T(8,128)(2,1)S(1)}, bf16[2304,384]{1,0:T(8,128)(2,1)S(1)}, s32[8,128]{1,0:T(8,128)S(1)}) custom-call(s32[8]{0:T(128)S(1)} %stack.48.refs_0_, f32[2]{0:T(128)S(1)} %maximum_divide_fusion.refs_1_, bf16[384,4608]{1,0:T(8,128)(2,1)S(1)} %copy-done.8, ...), custom_call_target="tpu_custom_call" | custom-call | flops 30000001024 | tf_op jit(solution)/shard_map/pallas_call | solution.py:112
  25.3 2.1 %collective-permute-start.7 = (f32[288,1024]{1,0:T(8,128)S(1)}, f32[288,1024]{1,0:T(8,128)S(1)}, u32[]{:S(2)}, u32[]{:S(2)}) collective-permute-start(f32[288,1024]{1,0:T(8,128)S(1)} %get-tuple-element.103.refs_1_), channel_id=1, source_target_pairs={{0,16},{8,24},{16,0},{24,8},{1,17},{9,25},{17,1},{25,9},{2,18},{10... | collective-permute-start | bytes 3538952 | tf_op jit(solution)/shard_map/ppermute | solution.py:554
  28.9 2.8 %collective-permute-done.2.refs_2_.refs_1_ = bf16[576,384]{1,0:T(8,128)(2,1)S(1)} collective-permute-done((bf16[576,384]{1,0:T(8,128)(2,1)S(1)}, bf16[576,384]{1,0:T(8,128)(2,1)S(1)}, u32[]{:S(2)}, u32[]{:S(2)}) %collective-permute-start.2) | collective-permute-done | bytes 442400 | tf_op jit(solution)/shard_map/ppermute | solution.py:551
  31.7 2.3 %shard_map.140 = (bf16[576,1024]{1,0:T(8,128)(2,1)S(1)}, s32[8,128]{1,0:T(8,128)S(1)}) custom-call(s32[8]{0:T(128)S(1)} %stack.48.refs_0_, bf16[2304,384]{1,0:T(8,128)(2,1)S(1)} %get-tuple-element.90.refs_1_.refs_2_, bf16[576,384]{1,0:T(8,128)(2,1)S(1)} %collective-permute-done.2.refs_2_.refs_1_, bf16[384,1024]{1,0:T(8,128)(2,1)S(1)} %copy-done.3, ...), custom_call_target="tpu_custom_call" | custom-call | tf_op jit(solution)/shard_map/pallas_call | solution.py:112
  34.1 2.6 %collective-permute-done.1.refs_3_.refs_4_ = bf16[576,1024]{1,0:T(8,128)(2,1)S(1)} collective-permute-done((bf16[576,1024]{1,0:T(8,128)(2,1)S(1)}, bf16[576,1024]{1,0:T(8,128)(2,1)S(1)}, u32[]{:S(2)}, u32[]{:S(2)}) %collective-permute-start.1) | collective-permute-done | bytes 1179680 | tf_op jit(solution)/shard_map/ppermute | solution.py:545
  40.0 3.4 %shard_map.142 = (bf16[1728,384]{1,0:T(8,128)(2,1)S(1)}, bf16[1152,384]{1,0:T(8,128)(2,1)S(1)}, s32[8,128]{1,0:T(8,128)S(1)}) custom-call(s32[8]{0:T(128)S(1)} %stack.48.refs_0_, bf16[384,1024]{1,0:T(8,128)(2,1)S(1)} %copy-done.3, bf16[384,1024]{1,0:T(8,128)(2,1)S(1)} %collective-permute-done.refs_3_.refs_4_.refs_2_, ...), custom_call_target="tpu_custom_call", output_to_operand_aliasing={{0}: (5, {})} | custom-call | flops 12000000000 | tf_op jit(solution)/shard_map/pallas_call | solution.py:112
  44.0 2.5 %shard_map.143 = (f32[384,1024]{1,0:T(8,128)S(1)}, s32[8,128]{1,0:T(8,128)S(1)}) custom-call(s32[8]{0:T(128)S(1)} %stack.48.refs_0_, bf16[2304,384]{1,0:T(8,128)(2,1)S(1)} %get-tuple-element.90.refs_1_.refs_2_, bf16[2304,384]{1,0:T(8,128)(2,1)S(1)} %get-tuple-element.90.refs_1_.refs_2_, bf16[576,1024]{1,0:T(8,128)(2,1)S(1)} %collective-permute-done.1.refs_3_.refs_4_, ...), custom_call_target="tpu_custom_call" | custom-call | tf_op jit(solution)/shard_map/pallas_call | solution.py:112
  46.5 5.2 %collective-permute-done.7.refs_2_ = f32[288,1024]{1,0:T(8,128)S(1)} collective-permute-done((f32[288,1024]{1,0:T(8,128)S(1)}, f32[288,1024]{1,0:T(8,128)S(1)}, u32[]{:S(2)}, u32[]{:S(2)}) %collective-permute-start.7) | collective-permute-done | bytes 1179680 | tf_op jit(solution)/shard_map/ppermute | solution.py:554
  52.5 2.3 %shard_map.145 = (bf16[576,1024]{1,0:T(8,128)(2,1)S(1)}, s32[8,128]{1,0:T(8,128)S(1)}) custom-call(s32[8]{0:T(128)S(1)} %stack.48.refs_0_, bf16[2304,384]{1,0:T(8,128)(2,1)S(1)} %get-tuple-element.90.refs_1_.refs_2_, bf16[1152,384]{1,0:T(8,128)(2,1)S(1)} %collective-permute-done.6.refs_2_.refs_1_, bf16[384,1024]{1,0:T(8,128)(2,1)S(1)} %copy-done.3, ...), custom_call_target="tpu_custom_call" | custom-call | flops 30000001024 | tf_op jit(solution)/shard_map/pallas_call | solution.py:112
  54.8 2.4 %shard_map.146 = (f32[576,1024]{1,0:T(8,128)S(1)}, s32[8,128]{1,0:T(8,128)S(1)}) custom-call(s32[8]{0:T(128)S(1)} %stack.48.refs_0_, bf16[2304,384]{1,0:T(8,128)(2,1)S(1)} %get-tuple-element.90.refs_1_.refs_2_, bf16[1152,384]{1,0:T(8,128)(2,1)S(1)} %collective-permute-done.6.refs_2_.refs_1_, bf16[384,1024]{1,0:T(8,128)(2,1)S(1)} %copy-done.3, ...), custom_call_target="tpu_custom_call" | custom-call | flops 1000000000 | tf_op jit(solution)/shard_map/pallas_call | solution.py:112
  57.3 3.9 %shard_map.147 = (f32[576,1024]{1,0:T(8,128)}, f32[576,1024]{1,0:T(8,128)}, f32[576,1024]{1,0:T(8,128)S(1)}, s32[8,128]{1,0:T(8,128)S(1)}) custom-call(s32[8]{0:T(128)S(1)} %stack.48.refs_0_, f32[288,1024]{1,0:T(8,128)S(1)} %get-tuple-element.110.refs_1_, f32[288,1024]{1,0:T(8,128)S(1)} %collective-permute-done.10.refs_2_, f32[576,1024]{1,0:T(8,128)S(1)} %copy-done, ...), custom_call_target="tpu_custom_call" | custom-call | flops 1000000000 | tf_op jit(solution)/shard_map/pallas_call | solution.py:112
  61.2 2.9 %collective-permute-done.8.refs_2_.refs_4_ = bf16[576,1024]{1,0:T(8,128)(2,1)S(1)} collective-permute-done((bf16[576,1024]{1,0:T(8,128)(2,1)S(1)}, bf16[576,1024]{1,0:T(8,128)(2,1)S(1)}, u32[]{:S(2)}, u32[]{:S(2)}) %collective-permute-start.8) | collective-permute-done | bytes 1179680 | tf_op jit(solution)/shard_map/ppermute | solution.py:545
  65.4 3.7 %collective-permute-start.13 = (bf16[384,1024]{1,0:T(8,128)(2,1)S(1)}, bf16[384,1024]{1,0:T(8,128)(2,1)S(1)}, u32[]{:S(2)}, u32[]{:S(2)}) collective-permute-start(bf16[384,1024]{1,0:T(8,128)(2,1)S(1)} %get-tuple-element.117), channel_id=1, source_target_pairs={{0,2},{1,3},{2,0},{3,1},{4,6},{5,7},{6,4},{7,5},{8,10},{9,11},{10,... | collective-permute-start | bytes 2359304 | tf_op jit(solution)/shard_map/ppermute | solution.py:545
  69.8 2.0 %shard_map.149 = (bf16[576,384]{1,0:T(8,128)(2,1)S(1)}, bf16[576,384]{1,0:T(8,128)(2,1)S(1)}, bf16[576,1024]{1,0:T(8,128)(2,1)S(1)}, s32[8,128]{1,0:T(8,128)S(1)}) custom-call(s32[8]{0:T(128)S(1)} %stack.48.refs_0_, bf16[384,1024]{1,0:T(8,128)(2,1)S(1)} %copy-done.3, bf16[384,1024]{1,0:T(8,128)(2,1)S(1)} %collective-permute-done.refs_3_.refs_4_.refs_2_, ...), custom_call_target="tpu_custom_call" | custom-call | tf_op jit(solution)/shard_map/pallas_call | solution.py:112
  72.4 2.1 %collective-permute-start.11 = (bf16[192,1024]{1,0:T(8,128)(2,1)S(1)}, bf16[192,1024]{1,0:T(8,128)(2,1)S(1)}, u32[]{:S(2)}, u32[]{:S(2)}) collective-permute-start(bf16[192,1024]{1,0:T(8,128)(2,1)S(1)} %get-tuple-element.114), channel_id=1, source_target_pairs={{0,2},{1,3},{2,0},{3,1},{4,6},{5,7},{6,4},{7,5},{8,10},{9,11},{10,... | collective-permute-start | bytes 1179656 | tf_op jit(solution)/shard_map/ppermute | solution.py:545
  74.4 2.5 %shard_map.150 = (f32[384,1024]{1,0:T(8,128)S(1)}, s32[8,128]{1,0:T(8,128)S(1)}) custom-call(s32[8]{0:T(128)S(1)} %stack.48.refs_0_, bf16[1152,384]{1,0:T(8,128)(2,1)S(1)} %collective-permute-done.6.refs_2_.refs_1_, bf16[1152,384]{1,0:T(8,128)(2,1)S(1)} %collective-permute-done.6.refs_2_.refs_1_, bf16[576,1024]{1,0:T(8,128)(2,1)S(1)} %get-tuple-element.120.refs_3_.refs_2_, ...), custom_call_target="tpu_custom_call" | custom-call | tf_op jit(solution)/shard_map/pallas_call | solution.py:112
  76.9 1.9 %shard_map.151 = (f32[384,1024]{1,0:T(8,128)S(1)}, s32[8,128]{1,0:T(8,128)S(1)}) custom-call(s32[8]{0:T(128)S(1)} %stack.48.refs_0_, bf16[2304,384]{1,0:T(8,128)(2,1)S(1)} %get-tuple-element.90.refs_1_.refs_2_, bf16[576,1024]{1,0:T(8,128)(2,1)S(1)} %get-tuple-element.120.refs_3_.refs_2_, f32[384,1024]{1,0:T(8,128)S(1)} %get-tuple-element.121.refs_3_, ...), custom_call_target="tpu_custom_call" | custom-call | tf_op jit(solution)/shard_map/pallas_call | solution.py:112
  79.8 4.1 %shard_map.152 = (bf16[384,4608]{1,0:T(8,128)(2,1)}, s32[8,128]{1,0:T(8,128)S(1)}) custom-call(s32[8]{0:T(128)S(1)} %stack.48.refs_0_, bf16[1152,384]{1,0:T(8,128)(2,1)S(1)} %get-tuple-element.118.refs_1_.refs_2_, bf16[1152,384]{1,0:T(8,128)(2,1)S(1)} %get-tuple-element.118.refs_1_.refs_2_, ...), custom_call_target="tpu_custom_call" | custom-call | tf_op jit(solution)/shard_map/pallas_call | solution.py:112
  83.9 3.7 %collective-permute-done.13.refs_4_.refs_2_ = bf16[384,1024]{1,0:T(8,128)(2,1)S(1)} collective-permute-done((bf16[384,1024]{1,0:T(8,128)(2,1)S(1)}, bf16[384,1024]{1,0:T(8,128)(2,1)S(1)}, u32[]{:S(2)}, u32[]{:S(2)}) %collective-permute-start.13) | collective-permute-done | bytes 786464 | tf_op jit(solution)/shard_map/ppermute | solution.py:545
  90.6 2.3 %collective-permute-start.21 = (bf16[384,1024]{1,0:T(8,128)(2,1)S(1)}, bf16[384,1024]{1,0:T(8,128)(2,1)S(1)}, u32[]{:S(2)}, u32[]{:S(2)}) collective-permute-start(bf16[384,1024]{1,0:T(8,128)(2,1)S(1)} %get-tuple-element.148), channel_id=1, source_target_pairs={{0,2},{1,3},{2,0},{3,1},{4,6},{5,7},{6,4},{7,5},{8,10},{9,11},{10,... | collective-permute-start | bytes 2359304 | tf_op jit(solution)/shard_map/ppermute | solution.py:545
  93.8 1.9 %shard_map.155 = (f32[384,1024]{1,0:T(8,128)S(1)}, s32[8,128]{1,0:T(8,128)S(1)}) custom-call(s32[8]{0:T(128)S(1)} %stack.48.refs_0_, bf16[1728,384]{1,0:T(8,128)(2,1)S(1)} %collective-permute-done.5.refs_3_.refs_4_.refs_5_.refs_1_.refs_2_, bf16[576,1024]{1,0:T(8,128)(2,1)S(1)} %get-tuple-element.91.refs_3_.refs_4_.refs_2_, ...), custom_call_target="tpu_custom_call" | custom-call | tf_op jit(solution)/shard_map/pallas_call | solution.py:112
  101.0 2.8 %collective-permute-done.17.refs_6_ = bf16[192,384]{1,0:T(8,128)(2,1)S(1)} collective-permute-done((bf16[192,384]{1,0:T(8,128)(2,1)S(1)}, bf16[192,384]{1,0:T(8,128)(2,1)S(1)}, u32[]{:S(2)}, u32[]{:S(2)}) %collective-permute-start.17) | collective-permute-done | bytes 147488 | tf_op jit(solution)/shard_map/ppermute | solution.py:551
  104.6 1.9 %collective-permute-start.18 = (bf16[192,1024]{1,0:T(8,128)(2,1)S(1)}, bf16[192,1024]{1,0:T(8,128)(2,1)S(1)}, u32[]{:S(2)}, u32[]{:S(2)}) collective-permute-start(bf16[192,1024]{1,0:T(8,128)(2,1)S(1)} %get-tuple-element.141), channel_id=1, source_target_pairs={{0,2},{1,3},{2,0},{3,1},{4,6},{5,7},{6,4},{7,5},{8,10},{9,11},{10,... | collective-permute-start | bytes 1179656 | tf_op jit(solution)/shard_map/ppermute | solution.py:545
  107.2 2.4 %shard_map.159 = (f32[576,1024]{1,0:T(8,128)S(1)}, s32[8,128]{1,0:T(8,128)S(1)}) custom-call(s32[8]{0:T(128)S(1)} %stack.48.refs_0_, bf16[2304,384]{1,0:T(8,128)(2,1)S(1)} %get-tuple-element.90.refs_1_.refs_2_, bf16[1728,384]{1,0:T(8,128)(2,1)S(1)} %collective-permute-done.5.refs_3_.refs_4_.refs_5_.refs_1_.refs_2_, bf16[384,1024]{1,0:T(8,128)(2,1)S(1)} %copy-done.3, ...), custom_call_target="tpu_custom_call" | custom-call | tf_op jit(solution)/shard_map/pallas_call | solution.py:112
  109.6 1.9 %shard_map.160 = (f32[384,1024]{1,0:T(8,128)S(1)}, s32[8,128]{1,0:T(8,128)S(1)}) custom-call(s32[8]{0:T(128)S(1)} %stack.48.refs_0_, bf16[2304,384]{1,0:T(8,128)(2,1)S(1)} %get-tuple-element.90.refs_1_.refs_2_, bf16[2304,384]{1,0:T(8,128)(2,1)S(1)} %get-tuple-element.90.refs_1_.refs_2_, bf16[384,1024]{1,0:T(8,128)(2,1)S(1)} %get-tuple-element.134.refs_3_, ...), custom_call_target="tpu_custom_call" | custom-call | tf_op jit(solution)/shard_map/pallas_call | solution.py:112
  111.5 4.1 %shard_map.161 = (bf16[384,4608]{1,0:T(8,128)(2,1)}, s32[8,128]{1,0:T(8,128)S(1)}) custom-call(s32[8]{0:T(128)S(1)} %stack.48.refs_0_, bf16[576,384]{1,0:T(8,128)(2,1)S(1)} %get-tuple-element.150.refs_1_, bf16[384,384]{1,0:T(8,128)(2,1)S(1)} %get-tuple-element.151.refs_2_, ...), custom_call_target="tpu_custom_call", output_to_operand_aliasing={{0}: (7, {})} | custom-call | tf_op jit(solution)/shard_map/pallas_call | solution.py:112
  115.6 3.4 %shard_map.162 = (f32[576,1024]{1,0:T(8,128)}, f32[576,1024]{1,0:T(8,128)}, f32[576,1024]{1,0:T(8,128)}, s32[8,128]{1,0:T(8,128)S(1)}) custom-call(s32[8]{0:T(128)S(1)} %stack.48.refs_0_, f32[2]{0:T(128)S(1)} %maximum_divide_fusion.refs_1_, f32[576,1024]{1,0:T(8,128)S(1)} %get-tuple-element.140.refs_2_, ...), custom_call_target="tpu_custom_call" | custom-call | flops 12000000000 | tf_op jit(solution)/shard_map/pallas_call | solution.py:112
  119.0 2.6 %shard_map.163 = (f32[576,1024]{1,0:T(8,128)}, f32[576,1024]{1,0:T(8,128)}, f32[576,1024]{1,0:T(8,128)}, bf16[384,1024]{1,0:T(8,128)(2,1)}, s32[8,128]{1,0:T(8,128)}) custom-call(s32[8]{0:T(128)S(1)} %stack.48.refs_0_, f32[2]{0:T(128)S(1)} %maximum_divide_fusion.refs_1_, ...), custom_call_target="tpu_custom_call", output_to_operand_aliasing={{0}: (10, {}), {1}: (11, {}), {2}: (12, {})} | custom-call | tf_op jit(solution)/shard_map/pallas_call | solution.py:112
  (63 shorter events, 27.1 us)
Async XLA Ops:
  0.6 21.6 %collective-permute-start = (bf16[384,1024]{1,0:T(8,128)(2,1)}, bf16[384,1024]{1,0:T(8,128)(2,1)S(1)}, u32[]{:S(2)}, u32[]{:S(2)}) collective-permute-start(bf16[384,1024]{1,0:T(8,128)(2,1)} %refs_3_.11), channel_id=1, source_target_pairs={{0,1},{1,0},{2,3},{3,2},{4,5},{5,4},{6,7},{7,6},{8,9},{9,8},{10,11... | collective-permute-start | bytes 2359304 | tf_op jit(solution)/shard_map/ppermute | solution.py:551
  3.7 1.7 %copy-start.1 = (f32[1,576,1024]{2,1,0:T(8,128)S(1)}, f32[1,576,1024]{2,1,0:T(8,128)}, u32[]{:S(2)}) copy-start(f32[1,576,1024]{2,1,0:T(8,128)} %param.10) | copy-start | bytes 7077892
  5.4 9.3 %copy-start.2 = (f32[1,576,1024]{2,1,0:T(8,128)S(1)}, f32[1,576,1024]{2,1,0:T(8,128)}, u32[]{:S(2)}) copy-start(f32[1,576,1024]{2,1,0:T(8,128)} %param.10) | copy-start | bytes 7077892
  6.1 27.9 %collective-permute-start.4 = (bf16[576,1024]{1,0:T(8,128)(2,1)S(1)}, bf16[576,1024]{1,0:T(8,128)(2,1)S(1)}, u32[]{:S(2)}, u32[]{:S(2)}) collective-permute-start(bf16[576,1024]{1,0:T(8,128)(2,1)S(1)} %get-tuple-element.91.refs_3_.refs_4_.refs_2_), channel_id=1, source_target_pairs={{2,4},{3,5},{4,2},{5,3},{10,12},{11,13},{12,10},{13,11},{18,20},{1... | collective-permute-start | bytes 3538952 | tf_op jit(solution)/shard_map/ppermute | solution.py:545
  6.9 29.8 %collective-permute-start.1 = (bf16[576,1024]{1,0:T(8,128)(2,1)S(1)}, bf16[576,1024]{1,0:T(8,128)(2,1)S(1)}, u32[]{:S(2)}, u32[]{:S(2)}) collective-permute-start(bf16[576,1024]{1,0:T(8,128)(2,1)S(1)} %get-tuple-element.91.refs_3_.refs_4_.refs_2_), channel_id=1, source_target_pairs={{0,2},{1,3},{2,0},{3,1},{4,6},{5,7},{6,4},{7,5},{8,10},{9,11},{10,... | collective-permute-start | bytes 3538952 | tf_op jit(solution)/shard_map/ppermute | solution.py:545
  11.3 2.0 %copy-start.7 = (bf16[384,4608]{1,0:T(8,128)(2,1)S(1)}, bf16[384,4608]{1,0:T(8,128)(2,1)}, u32[]{:S(2)}) copy-start(bf16[384,4608]{1,0:T(8,128)(2,1)} %refs_2_.1) | copy-start | bytes 10616836
  13.3 1.7 %copy-start = (f32[576,1024]{1,0:T(8,128)S(1)}, f32[576,1024]{1,0:T(8,128)}, u32[]{:S(2)}) copy-start(f32[576,1024]{1,0:T(8,128)} %refs_3_.10) | copy-start | bytes 7077892
  14.1 17.6 %collective-permute-start.2 = (bf16[576,384]{1,0:T(8,128)(2,1)S(1)}, bf16[576,384]{1,0:T(8,128)(2,1)S(1)}, u32[]{:S(2)}, u32[]{:S(2)}) collective-permute-start(bf16[576,384]{1,0:T(8,128)(2,1)S(1)} %get-tuple-element.93), channel_id=1, source_target_pairs={{0,1},{1,0},{2,3},{3,2},{4,5},{5,4},{6,7},{7,6},{8,9},{9,8},{10,11... | collective-permute-start | bytes 1327112 | tf_op jit(solution)/shard_map/ppermute | solution.py:551
  14.9 7.3 %copy-start.8 = (bf16[384,4608]{1,0:T(8,128)(2,1)S(1)}, bf16[384,4608]{1,0:T(8,128)(2,1)}, u32[]{:S(2)}) copy-start(bf16[384,4608]{1,0:T(8,128)(2,1)} %refs_2_.1) | copy-start | bytes 10616836
  15.8 8.7 %collective-permute-start.3 = (f32[288,1024]{1,0:T(8,128)S(1)}, f32[288,1024]{1,0:T(8,128)S(1)}, u32[]{:S(2)}, u32[]{:S(2)}) collective-permute-start(f32[288,1024]{1,0:T(8,128)S(1)} %get-tuple-element.95), channel_id=1, source_target_pairs={{0,8},{8,0},{16,24},{24,16},{1,9},{9,1},{17,25},{25,17},{2,10},{10... | collective-permute-start | bytes 3538952 | tf_op jit(solution)/shard_map/ppermute | solution.py:554
  24.5 7.2 %copy-start.3 = (bf16[384,1024]{1,0:T(8,128)(2,1)S(1)}, bf16[384,1024]{1,0:T(8,128)(2,1)}, u32[]{:S(2)}) copy-start(bf16[384,1024]{1,0:T(8,128)(2,1)} %refs_3_.11) | copy-start | bytes 2359300
  25.3 26.4 %collective-permute-start.7 = (f32[288,1024]{1,0:T(8,128)S(1)}, f32[288,1024]{1,0:T(8,128)S(1)}, u32[]{:S(2)}, u32[]{:S(2)}) collective-permute-start(f32[288,1024]{1,0:T(8,128)S(1)} %get-tuple-element.103.refs_1_), channel_id=1, source_target_pairs={{0,16},{8,24},{16,0},{24,8},{1,17},{9,25},{17,1},{25,9},{2,18},{10... | collective-permute-start | bytes 3538952 | tf_op jit(solution)/shard_map/ppermute | solution.py:554
  27.4 25.1 %collective-permute-start.6 = (bf16[1152,384]{1,0:T(8,128)(2,1)S(1)}, bf16[1152,384]{1,0:T(8,128)(2,1)S(1)}, u32[]{:S(2)}, u32[]{:S(2)}) collective-permute-start(bf16[1152,384]{1,0:T(8,128)(2,1)S(1)} %get-tuple-element.102), channel_id=1, source_target_pairs={{0,1},{1,0},{2,3},{3,2},{4,5},{5,4},{6,7},{7,6},{8,9},{9,8},{10,11... | collective-permute-start | bytes 2654216 | tf_op jit(solution)/shard_map/ppermute | solution.py:551
  37.5 26.6 %collective-permute-start.8 = (bf16[576,1024]{1,0:T(8,128)(2,1)S(1)}, bf16[576,1024]{1,0:T(8,128)(2,1)S(1)}, u32[]{:S(2)}, u32[]{:S(2)}) collective-permute-start(bf16[576,1024]{1,0:T(8,128)(2,1)S(1)} %get-tuple-element.108), channel_id=1, source_target_pairs={{0,2},{1,3},{2,0},{3,1},{4,6},{5,7},{6,4},{7,5},{8,10},{9,11},{10,... | collective-permute-start | bytes 3538952 | tf_op jit(solution)/shard_map/ppermute | solution.py:545
  39.3 24.8 %collective-permute-start.9 = (bf16[576,1024]{1,0:T(8,128)(2,1)S(1)}, bf16[576,1024]{1,0:T(8,128)(2,1)S(1)}, u32[]{:S(2)}, u32[]{:S(2)}) collective-permute-start(bf16[576,1024]{1,0:T(8,128)(2,1)S(1)} %get-tuple-element.109), channel_id=1, source_target_pairs={{2,4},{3,5},{4,2},{5,3},{10,12},{11,13},{12,10},{13,11},{18,20},{1... | collective-permute-start | bytes 3538952 | tf_op jit(solution)/shard_map/ppermute | solution.py:545
  43.4 35.7 %collective-permute-start.5 = (bf16[1728,384]{1,0:T(8,128)(2,1)S(1)}, bf16[1728,384]{1,0:T(8,128)(2,1)S(1)}, u32[]{:S(2)}, u32[]{:S(2)}) collective-permute-start(bf16[1728,384]{1,0:T(8,128)(2,1)S(1)} %get-tuple-element.101), channel_id=1, source_target_pairs={{0,1},{1,0},{2,3},{3,2},{4,5},{5,4},{6,7},{7,6},{8,9},{9,8},{10,11... | collective-permute-start | bytes 3981320 | tf_op jit(solution)/shard_map/ppermute | solution.py:551
  52.4 4.8 %collective-permute-start.10 = (f32[288,1024]{1,0:T(8,128)S(1)}, f32[288,1024]{1,0:T(8,128)S(1)}, u32[]{:S(2)}, u32[]{:S(2)}) collective-permute-start(f32[288,1024]{1,0:T(8,128)S(1)} %get-tuple-element.110.refs_1_), channel_id=1, source_target_pairs={{0,8},{8,0},{16,24},{24,16},{1,9},{9,1},{17,25},{25,17},{2,10},{10... | collective-permute-start | bytes 3538952 | tf_op jit(solution)/shard_map/ppermute | solution.py:554
  54.8 2.4 %copy-start.4 = (f32[576,1024]{1,0:T(8,128)S(1)}, f32[576,1024]{1,0:T(8,128)}, u32[]{:S(2)}) copy-start(f32[576,1024]{1,0:T(8,128)} %refs_4_.1) | copy-start | bytes 7077892
  65.4 22.1 %collective-permute-start.13 = (bf16[384,1024]{1,0:T(8,128)(2,1)S(1)}, bf16[384,1024]{1,0:T(8,128)(2,1)S(1)}, u32[]{:S(2)}, u32[]{:S(2)}) collective-permute-start(bf16[384,1024]{1,0:T(8,128)(2,1)S(1)} %get-tuple-element.117), channel_id=1, source_target_pairs={{0,2},{1,3},{2,0},{3,1},{4,6},{5,7},{6,4},{7,5},{8,10},{9,11},{10,... | collective-permute-start | bytes 2359304 | tf_op jit(solution)/shard_map/ppermute | solution.py:545
  69.1 20.6 %collective-permute-start.16 = (bf16[384,1024]{1,0:T(8,128)(2,1)S(1)}, bf16[384,1024]{1,0:T(8,128)(2,1)S(1)}, u32[]{:S(2)}, u32[]{:S(2)}) collective-permute-start(bf16[384,1024]{1,0:T(8,128)(2,1)S(1)} %get-tuple-element.129), channel_id=1, source_target_pairs={{2,4},{3,5},{4,2},{5,3},{10,12},{11,13},{12,10},{13,11},{18,20},{1... | collective-permute-start | bytes 2359304 | tf_op jit(solution)/shard_map/ppermute | solution.py:545
  71.8 21.1 %collective-permute-start.15 = (bf16[576,384]{1,0:T(8,128)(2,1)S(1)}, bf16[576,384]{1,0:T(8,128)(2,1)S(1)}, u32[]{:S(2)}, u32[]{:S(2)}) collective-permute-start(bf16[576,384]{1,0:T(8,128)(2,1)S(1)} %get-tuple-element.128), channel_id=1, source_target_pairs={{0,1},{1,0},{2,3},{3,2},{4,5},{5,4},{6,7},{7,6},{8,9},{9,8},{10,11... | collective-permute-start | bytes 1327112 | tf_op jit(solution)/shard_map/ppermute | solution.py:551
  72.4 23.4 %collective-permute-start.11 = (bf16[192,1024]{1,0:T(8,128)(2,1)S(1)}, bf16[192,1024]{1,0:T(8,128)(2,1)S(1)}, u32[]{:S(2)}, u32[]{:S(2)}) collective-permute-start(bf16[192,1024]{1,0:T(8,128)(2,1)S(1)} %get-tuple-element.114), channel_id=1, source_target_pairs={{0,2},{1,3},{2,0},{3,1},{4,6},{5,7},{6,4},{7,5},{8,10},{9,11},{10,... | collective-permute-start | bytes 1179656 | tf_op jit(solution)/shard_map/ppermute | solution.py:545
  79.1 19.2 %collective-permute-start.12 = (bf16[192,1024]{1,0:T(8,128)(2,1)S(1)}, bf16[192,1024]{1,0:T(8,128)(2,1)S(1)}, u32[]{:S(2)}, u32[]{:S(2)}) collective-permute-start(bf16[192,1024]{1,0:T(8,128)(2,1)S(1)} %get-tuple-element.116), channel_id=1, source_target_pairs={{2,4},{3,5},{4,2},{5,3},{10,12},{11,13},{12,10},{13,11},{18,20},{1... | collective-permute-start | bytes 1179656 | tf_op jit(solution)/shard_map/ppermute | solution.py:545
  89.1 14.7 %collective-permute-start.14 = (bf16[384,384]{1,0:T(8,128)(2,1)S(1)}, bf16[384,384]{1,0:T(8,128)(2,1)S(1)}, u32[]{:S(2)}, u32[]{:S(2)}) collective-permute-start(bf16[384,384]{1,0:T(8,128)(2,1)S(1)} %get-tuple-element.126), channel_id=1, source_target_pairs={{0,1},{1,0},{2,3},{3,2},{4,5},{5,4},{6,7},{7,6},{8,9},{9,8},{10,11... | collective-permute-start | bytes 884744 | tf_op jit(solution)/shard_map/ppermute | solution.py:551
  90.6 25.0 %collective-permute-start.21 = (bf16[384,1024]{1,0:T(8,128)(2,1)S(1)}, bf16[384,1024]{1,0:T(8,128)(2,1)S(1)}, u32[]{:S(2)}, u32[]{:S(2)}) collective-permute-start(bf16[384,1024]{1,0:T(8,128)(2,1)S(1)} %get-tuple-element.148), channel_id=1, source_target_pairs={{0,2},{1,3},{2,0},{3,1},{4,6},{5,7},{6,4},{7,5},{8,10},{9,11},{10,... | collective-permute-start | bytes 2359304 | tf_op jit(solution)/shard_map/ppermute | solution.py:545
  92.9 22.7 %collective-permute-start.22 = (bf16[384,1024]{1,0:T(8,128)(2,1)S(1)}, bf16[384,1024]{1,0:T(8,128)(2,1)S(1)}, u32[]{:S(2)}, u32[]{:S(2)}) collective-permute-start(bf16[384,1024]{1,0:T(8,128)(2,1)S(1)} %get-tuple-element.149), channel_id=1, source_target_pairs={{2,4},{3,5},{4,2},{5,3},{10,12},{11,13},{12,10},{13,11},{18,20},{1... | collective-permute-start | bytes 2359304 | tf_op jit(solution)/shard_map/ppermute | solution.py:545
  97.0 6.9 %collective-permute-start.17 = (bf16[192,384]{1,0:T(8,128)(2,1)S(1)}, bf16[192,384]{1,0:T(8,128)(2,1)S(1)}, u32[]{:S(2)}, u32[]{:S(2)}) collective-permute-start(bf16[192,384]{1,0:T(8,128)(2,1)S(1)} %get-tuple-element.133), channel_id=1, source_target_pairs={{0,1},{1,0},{2,3},{3,2},{4,5},{5,4},{6,7},{7,6},{8,9},{9,8},{10,11... | collective-permute-start | bytes 442376 | tf_op jit(solution)/shard_map/ppermute | solution.py:551
  100.2 18.8 %collective-permute-start.20 = (bf16[384,1024]{1,0:T(8,128)(2,1)S(1)}, bf16[384,1024]{1,0:T(8,128)(2,1)S(1)}, u32[]{:S(2)}, u32[]{:S(2)}) collective-permute-start(bf16[384,1024]{1,0:T(8,128)(2,1)S(1)} %get-tuple-element.147), channel_id=1, source_target_pairs={{0,1},{1,0},{2,3},{3,2},{4,5},{5,4},{6,7},{7,6},{8,9},{9,8},{10,11... | collective-permute-start | bytes 2359304 | tf_op jit(solution)/shard_map/ppermute | solution.py:551
  104.6 14.4 %collective-permute-start.18 = (bf16[192,1024]{1,0:T(8,128)(2,1)S(1)}, bf16[192,1024]{1,0:T(8,128)(2,1)S(1)}, u32[]{:S(2)}, u32[]{:S(2)}) collective-permute-start(bf16[192,1024]{1,0:T(8,128)(2,1)S(1)} %get-tuple-element.141), channel_id=1, source_target_pairs={{0,2},{1,3},{2,0},{3,1},{4,6},{5,7},{6,4},{7,5},{8,10},{9,11},{10,... | collective-permute-start | bytes 1179656 | tf_op jit(solution)/shard_map/ppermute | solution.py:545
  106.5 12.5 %collective-permute-start.19 = (bf16[192,1024]{1,0:T(8,128)(2,1)S(1)}, bf16[192,1024]{1,0:T(8,128)(2,1)S(1)}, u32[]{:S(2)}, u32[]{:S(2)}) collective-permute-start(bf16[192,1024]{1,0:T(8,128)(2,1)S(1)} %get-tuple-element.142), channel_id=1, source_target_pairs={{2,4},{3,5},{4,2},{5,3},{10,12},{11,13},{12,10},{13,11},{18,20},{1... | collective-permute-start | bytes 1179656 | tf_op jit(solution)/shard_map/ppermute | solution.py:545
  111.5 4.1 %copy-start.5 = (f32[1,576,1024]{2,1,0:T(8,128)S(1)}, f32[1,576,1024]{2,1,0:T(8,128)}, u32[]{:S(2)}) copy-start(f32[1,576,1024]{2,1,0:T(8,128)} %param.11) | copy-start | bytes 7077892
  111.5 4.1 %copy-start.6 = (f32[1,576,1024]{2,1,0:T(8,128)S(1)}, f32[1,576,1024]{2,1,0:T(8,128)}, u32[]{:S(2)}) copy-start(f32[1,576,1024]{2,1,0:T(8,128)} %param.12) | copy-start | bytes 7077892
